TPU v7x, 256 devices: a whole 4x4x8 slice. The times are simulated.
256 devices in a mesh: tile: 8 (over z), dp: 32 (over x, y, core).
Axes of the slice: x: 4, y: 4, z: 8, core: 2. Of those that a mesh axis runs over, the one named last changes fastest.
Arguments:
- inputs: bfloat16 [32, 64, 288, 256], P('dp', 'tile'), may hold values from -6 to 6
- pre_first: bfloat16 [32, 64, 288, 256], P('dp', 'tile'), may hold values from -6 to 6
- pre_second: bfloat16 [32, 64, 288, 256], P('dp', 'tile'), may hold values from -6 to 6
- labels: int32 [32, 64, 288], P('dp', 'tile'), may hold values from 0 to 2
- classifier: bfloat16 [256, 3], replicated, may hold values from -0.375 to 0.375
- w_first: float32 [589824], P(('tile', 'dp')), may hold values from -0.125 to 0.125
- m_first: float32 [589824], P(('tile', 'dp')), may hold values from -48 to 48
- v_first: float32 [589824], P(('tile', 'dp')), may hold values from 0.589824 to 5.89824
- w_second: float32 [589824], P(('tile', 'dp')), may hold values from -0.125 to 0.125
- m_second: float32 [589824], P(('tile', 'dp')), may hold values from -48 to 48
- v_second: float32 [589824], P(('tile', 'dp')), may hold values from 0.589824 to 5.89824
Outputs:
- w_first_new: float32 [589824], P(('tile', 'dp'))
- m_first_new: float32 [589824], P(('tile', 'dp'))
- v_first_new: float32 [589824], P(('tile', 'dp'))
- w_second_new: float32 [589824], P(('tile', 'dp'))
- m_second_new: float32 [589824], P(('tile', 'dp'))
- v_second_new: float32 [589824], P(('tile', 'dp'))
- w_first_step: float32 [589824], P(('tile', 'dp'))
- w_second_step: float32 [589824], P(('tile', 'dp'))
All inputs are finite; a program needn't handle non-finite values.
Results may differ from a plain program's by a relative error of at most 0.0017.
Values may be sent and summed in bfloat16 or wider, within the bound.
A program may use at most 64 MiB of HBM per device.

v0:
```python
import jax
import jax.numpy as jnp
from jax import lax
from jax.sharding import PartitionSpec as P

STEP = 10


beta_one = 0.9
beta_two = 0.999
epsilon = 1e-06
weight_decay = 0.01
learn_rate = 0.002


def extended(cells, sides, width):
    for axis, dim in sides:
        count = lax.axis_size(axis)
        ends = count - 1
        head = lax.slice_in_dim(cells, 0, width, axis=dim)
        tail = lax.slice_in_dim(cells, cells.shape[dim] - width, cells.shape[dim], axis=dim)
        cells = jnp.concatenate(
            [
                lax.ppermute(tail, axis, [(i, (i + 1) % count) for i in range(ends)]),
                cells,
                lax.ppermute(head, axis, [((i + 1) % count, i) for i in range(ends)]),
            ],
            axis=dim,
        )
    return cells


def pad_cols(field):
    return jnp.pad(field, ((0, 0), (1, 1), (0, 0)))


def weight_terms(padded, grad):
    height, width, chans = grad.shape
    flat_grad = grad.reshape(-1, chans)
    terms = []
    for row_off in range(3):
        for col_off in range(3):
            window = padded[row_off : row_off + height, col_off : col_off + width].reshape(
                -1, chans
            )
            terms.append(
                lax.dot_general(
                    window, flat_grad, (((0,), (0,)), ((), ())), preferred_element_type=jnp.float32
                )
            )
    return jnp.stack(terms).reshape(-1)


def input_terms(padded, kernel):
    height = padded.shape[0] - 2
    width = padded.shape[1] - 2
    chans = padded.shape[2]
    total = jnp.zeros((height * width, chans), jnp.float32)
    for row_off in range(3):
        for col_off in range(3):
            window = padded[
                2 - row_off : 2 - row_off + height, 2 - col_off : 2 - col_off + width
            ].reshape(-1, chans)
            total = total + lax.dot_general(
                window,
                kernel[row_off, col_off],
                (((1,), (1,)), ((), ())),
                preferred_element_type=jnp.float32,
            )
    return total.reshape(height, width, chans)


def reduce_grad(term):
    return lax.psum_scatter(term, ("tile", "dp"), scatter_dimension=0, tiled=True)


def moments(grad, weight, first, second):
    first_new = beta_one * first + (1.0 - beta_one) * grad
    second_new = beta_two * second + (1.0 - beta_two) * grad * grad
    corr_one = 1.0 - beta_one**STEP
    corr_two = 1.0 - beta_two**STEP
    update = (
        first_new / corr_one / (jnp.sqrt(second_new / corr_two) + epsilon) + weight_decay * weight
    )
    return (first_new, second_new, update)


def body(
    inputs,
    pre_first,
    pre_second,
    labels,
    classifier,
    w_first,
    m_first,
    v_first,
    w_second,
    m_second,
    v_second,
):
    image = inputs[0]
    first_pre = pre_first[0]
    second_pre = pre_second[0]
    label = labels[0]
    chans = image.shape[-1]
    classes = classifier.shape[1]
    hidden = jnp.maximum(first_pre, jnp.zeros_like(first_pre))
    active = jnp.maximum(second_pre, jnp.zeros_like(second_pre))
    hidden_pad = pad_cols(extended(hidden, (("tile", 0),), 1))
    logits = jnp.dot(active.reshape(-1, chans), classifier, preferred_element_type=jnp.float32)
    expo = jnp.exp(logits)
    prob = expo / jnp.sum(expo, axis=1, keepdims=True)
    onehot = (label.reshape(-1, 1) == jnp.arange(classes, dtype=jnp.int32)[None, :]).astype(
        jnp.float32
    )
    dlogit = prob - onehot
    grad_act = jnp.dot(
        dlogit, classifier.astype(jnp.float32).T, precision=lax.Precision.HIGHEST
    ).reshape(second_pre.shape)
    grad_second = jnp.where(second_pre > 0, grad_act, jnp.zeros_like(grad_act)).astype(jnp.bfloat16)
    gw_second = reduce_grad(weight_terms(hidden_pad, grad_second))
    kernel = lax.all_gather(
        w_second.astype(jnp.bfloat16), ("tile", "dp"), axis=0, tiled=True
    ).reshape(3, 3, chans, chans)
    grad_pad = pad_cols(extended(grad_second, (("tile", 0),), 1))
    dhidden = input_terms(grad_pad, kernel)
    grad_first = jnp.where(first_pre > 0, dhidden, jnp.zeros_like(dhidden)).astype(jnp.bfloat16)
    image_pad = pad_cols(extended(image, (("tile", 0),), 1))
    gw_first = reduce_grad(weight_terms(image_pad, grad_first))
    m1n, v1n, upd_first = moments(gw_first, w_first, m_first, v_first)
    m2n, v2n, upd_second = moments(gw_second, w_second, m_second, v_second)
    sums = lax.psum(
        (
            jnp.sum(w_first * w_first),
            jnp.sum(upd_first * upd_first),
            jnp.sum(w_second * w_second),
            jnp.sum(upd_second * upd_second),
        ),
        ("tile", "dp"),
    )
    trust_first = jnp.sqrt(sums[0]) / jnp.sqrt(sums[1])
    trust_second = jnp.sqrt(sums[2]) / jnp.sqrt(sums[3])
    step_first = trust_first * upd_first
    step_second = trust_second * upd_second
    w1n = w_first - learn_rate * step_first
    w2n = w_second - learn_rate * step_second
    return (w1n, m1n, v1n, w2n, m2n, v2n, step_first, step_second)


def solution(mesh):
    in_specs = (
        P("dp", "tile", None, None),
        P("dp", "tile", None, None),
        P("dp", "tile", None, None),
        P("dp", "tile", None),
        P(),
        P(("tile", "dp")),
        P(("tile", "dp")),
        P(("tile", "dp")),
        P(("tile", "dp")),
        P(("tile", "dp")),
        P(("tile", "dp")),
    )
    out_specs = (
        P(("tile", "dp")),
        P(("tile", "dp")),
        P(("tile", "dp")),
        P(("tile", "dp")),
        P(("tile", "dp")),
        P(("tile", "dp")),
        P(("tile", "dp")),
        P(("tile", "dp")),
    )
    return jax.shard_map(body, mesh=mesh, in_specs=in_specs, out_specs=out_specs, check_vma=False)
```

profile of v0, /device:TPU:1, one launch (start us, length us, event | category | flops | bytes accessed | tf_op | source)
XLA Modules:
  0.0 520.1 jit_solution(3807071919693491767)
XLA Ops:
  7.2 1.4 broadcast_maximum_fusion.1
  9.2 1.2 fusion.142
  10.4 1.4 select_convert_fusion.3
  11.8 1.4 collective-permute-start.3
  13.2 5.0 collective-permute-start.2
  18.2 0.6 reshape.115
  18.9 1.0 slice_bitcast_fusion.3
  20.0 1.4 collective-permute-start.1
  21.6 1.3 collective-permute-start.5
  22.9 4.8 collective-permute-start.4
  28.1 1.1 collective-permute-done.5
  29.2 3.8 collective-permute-start
  33.9 0.5 fusion.125
  34.5 0.5 fusion.87
  35.6 0.5 fusion.114
  36.1 0.5 fusion.99
  36.6 0.5 fusion.105
  37.2 0.5 fusion.119
  37.7 0.5 fusion.111
  38.3 2.6 copy.25
  41.3 1.7 pad_maximum_fusion
  43.4 2.9 fusion.157
  46.3 80.8 %all-gather.3.cloned.1.call-done = bf16[256,1,2304]{2,1,0:T(2,128)(2,1)} async-done(((bf16[1,1,2304]{2,1,0:T(2,128)(2,1)}), bf16[256,1,2304]{2,1,0:T(2,128)(2,1)}) %all-gather.3.cloned.1.call-update) | async-done | bytes 1179664 | tf_op jit(solution)/shard_map/all_gather | solution.py:122
  127.1 9.4 %reduce = bf16[256,2304]{1,0:T(8,128)(2,1)} reduce(bf16[256,1,2304]{2,1,0:T(2,128)(2,1)} %all-gather.3.cloned.1.call-done, bf16[]{:T(256)} %constant.45), dimensions={1}, to_apply=%all-gather.reduce_sub_computation | reduce | bytes 2359298 | tf_op jit(solution)/shard_map/all_gather | solution.py:122
  136.5 3.4 reshape.104
  139.9 1.9 fusion.140
  142.4 0.8 copy-done.15
  143.7 0.7 copy-done.12
  144.9 0.8 copy-done.11
  146.2 0.7 copy-done.4
  147.5 0.8 copy-done.10
  148.7 0.8 copy-done.9
  150.0 0.7 copy-done.13
  151.3 0.6 select_convert_fusion.1
  152.4 0.7 copy-done.18
  153.1 0.5 fusion.137
  153.7 0.5 fusion.51
  155.2 0.6 fusion.115
  155.8 0.5 fusion.63
  156.4 0.5 fusion.69
  156.9 0.5 fusion.131
  157.4 0.5 fusion.75
  158.0 2.7 copy.24
  160.7 268.5 %all-reduce.9.cloned.1.call-done = (f32[589824]{0:T(1024)}, f32[589824]{0:T(1024)}) async-done(((f32[589824]{0:T(1024)}, f32[589824]{0:T(1024)}), (f32[589824]{0:T(1024)}, f32[589824]{0:T(1024)})) %all-reduce.9.cloned.1.call-update) | async-done | bytes 4718608
  429.2 2.0 multiply_reduce_fusion
  431.3 78.0 %all-reduce.5 = (f32[]{:T(128)}, f32[]{:T(128)}, f32[]{:T(128)}, f32[]{:T(128)}) all-reduce(f32[]{:T(128)} %get-tuple-element.50, f32[]{:T(128)} %get-tuple-element.51, f32[]{:T(128)} %get-tuple-element.46, f32[]{:T(128)} %get-tuple-element.18), channel_id=1, replica_groups=mesh['tile'=8,'dp'=32] {'tile','dp'}, use_global_device_ids=true, to_apply=%region_1.2 | all-reduce | flops 4 | bytes 32 | tf_op jit(solution)/shard_map/psum | solution.py:132
  512.0 0.6 multiply_subtract_fusion.1
  512.6 0.6 multiply_subtract_fusion
  (76 shorter events, 9.1 us)
Async XLA Ops:
  7.2 1.5 copy-start
  7.2 1.4 copy-start.21
  7.2 119.9 %all-gather.3.cloned.1.call-start = ((), (), s32[]{:S(2)}) async-start(), calls=%async_computation | async-start | bytes 2368512 | tf_op jit(solution)/shard_map/all_gather | solution.py:122
  8.6 1.7 copy-start.14
  10.3 1.4 copy-start.5
  10.3 7.9 %copy-start.19 = (f32[2304]{0:T(1024)S(1)}, f32[2304]{0:T(1024)}, u32[]{:S(2)}) copy-start(f32[2304]{0:T(1024)} %param.19) | copy-start | bytes 27652
  11.7 9.6 %copy-start.2 = (bf16[1,8,288,256]{3,2,1,0:T(8,128)(2,1)S(1)}, bf16[1,8,288,256]{3,2,1,0:T(8,128)(2,1)}, u32[]{:S(2)}) copy-start(bf16[1,8,288,256]{3,2,1,0:T(8,128)(2,1)} %param.12) | copy-start | bytes 3538948
  11.8 29.1 %collective-permute-start.3 = (bf16[1,288,256]{2,1,0:T(8,128)(2,1)S(1)}, bf16[1,288,256]{2,1,0:T(8,128)(2,1)S(1)}, u32[]{:S(2)}, u32[]{:S(2)}) collective-permute-start(bf16[1,288,256]{2,1,0:T(8,128)(2,1)S(1)} %get-tuple-element.45), channel_id=1, source_target_pairs={{32,0},{64,32},{96,64},{128,96},{160,128},{192,160},{224,192},{33,... | collective-permute-start | bytes 442376 | tf_op jit(solution)/shard_map/ppermute | solution.py:26
  13.2 27.7 %collective-permute-start.2 = (bf16[1,288,256]{2,1,0:T(8,128)(2,1)S(1)}, bf16[1,288,256]{2,1,0:T(8,128)(2,1)S(1)}, u32[]{:S(2)}, u32[]{:S(2)}) collective-permute-start(bf16[1,288,256]{2,1,0:T(8,128)(2,1)S(1)} %get-tuple-element.44), channel_id=1, source_target_pairs={{0,32},{32,64},{64,96},{96,128},{128,160},{160,192},{192,224},{1,3... | collective-permute-start | bytes 442376 | tf_op jit(solution)/shard_map/ppermute | solution.py:24
  18.9 410.3 %all-reduce.9.cloned.1.call-start = ((), (), s32[]{:S(2)}) async-start(), calls=%async_computation.1 | async-start | bytes 9437184
  19.9 7.8 %copy-start.6 = (bf16[2304,256]{1,0:T(8,128)(2,1)S(1)}, bf16[2304,256]{1,0:T(8,128)(2,1)}, u32[]{:S(2)}) copy-start(bf16[2304,256]{1,0:T(8,128)(2,1)} %copy-done.5) | copy-start | bytes 3538948
  19.9 7.8 %copy-start.16 = (pred[1,8,288,256]{3,2,1,0:T(8,128)(4,1)S(1)}, pred[1,8,288,256]{3,2,1,0:T(8,128)(4,1)}, u32[]{:S(2)}) copy-start(pred[1,8,288,256]{3,2,1,0:T(8,128)(4,1)} %get-tuple-element.29) | copy-start | bytes 1769476
  20.0 23.0 %collective-permute-start.1 = (bf16[1,288,256]{2,1,0:T(8,128)(2,1)S(1)}, bf16[1,288,256]{2,1,0:T(8,128)(2,1)S(1)}, u32[]{:S(2)}, u32[]{:S(2)}) collective-permute-start(bf16[1,288,256]{2,1,0:T(8,128)(2,1)S(1)} %get-tuple-element.41), channel_id=1, source_target_pairs={{32,0},{64,32},{96,64},{128,96},{160,128},{192,160},{224,192},{33,... | collective-permute-start | bytes 442376 | tf_op jit(solution)/shard_map/ppermute | solution.py:26
  21.6 7.6 %collective-permute-start.5 = (bf16[1,288,256]{2,1,0:T(8,128)(2,1)S(1)}, bf16[1,288,256]{2,1,0:T(8,128)(2,1)S(1)}, u32[]{:S(2)}, u32[]{:S(2)}) collective-permute-start(bf16[1,288,256]{2,1,0:T(8,128)(2,1)S(1)} %get-tuple-element.37), channel_id=1, source_target_pairs={{32,0},{64,32},{96,64},{128,96},{160,128},{192,160},{224,192},{33,... | collective-permute-start | bytes 442376 | tf_op jit(solution)/shard_map/ppermute | solution.py:26
  22.9 10.2 %collective-permute-start.4 = (bf16[1,288,256]{2,1,0:T(8,128)(2,1)S(1)}, bf16[1,288,256]{2,1,0:T(8,128)(2,1)S(1)}, u32[]{:S(2)}, u32[]{:S(2)}) collective-permute-start(bf16[1,288,256]{2,1,0:T(8,128)(2,1)S(1)} %get-tuple-element.36), channel_id=1, source_target_pairs={{0,32},{32,64},{64,96},{96,128},{128,160},{160,192},{192,224},{1,3... | collective-permute-start | bytes 442376 | tf_op jit(solution)/shard_map/ppermute | solution.py:24
  28.1 7.4 %copy-start.3 = (bf16[2304,256]{1,0:T(8,128)(2,1)}, bf16[2304,256]{1,0:T(8,128)(2,1)S(1)}, u32[]{:S(2)}) copy-start(bf16[2304,256]{1,0:T(8,128)(2,1)S(1)} %select_convert_fusion.2) | copy-start | bytes 3538948
  29.2 13.7 %collective-permute-start = (bf16[1,288,256]{2,1,0:T(8,128)(2,1)S(1)}, bf16[1,288,256]{2,1,0:T(8,128)(2,1)S(1)}, u32[]{:S(2)}, u32[]{:S(2)}) collective-permute-start(bf16[1,288,256]{2,1,0:T(8,128)(2,1)S(1)} %get-tuple-element.40), channel_id=1, source_target_pairs={{0,32},{32,64},{64,96},{96,128},{128,160},{160,192},{192,224},{1,3... | collective-permute-start | bytes 442376 | tf_op jit(solution)/shard_map/ppermute | solution.py:24
  41.3 1.7 copy-start.17
  139.9 1.9 copy-start.7
  139.9 2.0 copy-start.8
  141.9 1.3 copy-start.15
  143.2 1.3 copy-start.12
  144.4 1.3 copy-start.11
  145.7 1.3 copy-start.4
  147.0 1.3 copy-start.10
  148.2 1.3 copy-start.9
  149.5 1.3 copy-start.13
  151.9 1.3 copy-start.18
  160.7 268.5 %copy-start.20 = (f32[2304]{0:T(1024)S(1)}, f32[2304]{0:T(1024)}, u32[]{:S(2)}) copy-start(f32[2304]{0:T(1024)} %param.16) | copy-start | bytes 27652
  160.7 268.5 %copy-start.22 = (f32[2304]{0:T(1024)S(1)}, f32[2304]{0:T(1024)}, u32[]{:S(2)}) copy-start(f32[2304]{0:T(1024)} %param.20) | copy-start | bytes 27652
  160.7 268.5 %copy-start.23 = (f32[2304]{0:T(1024)S(1)}, f32[2304]{0:T(1024)}, u32[]{:S(2)}) copy-start(f32[2304]{0:T(1024)} %param.21) | copy-start | bytes 27652
  160.7 268.6 %copy-start.24 = (f32[2304]{0:T(1024)S(1)}, f32[2304]{0:T(1024)}, u32[]{:S(2)}) copy-start(f32[2304]{0:T(1024)} %param.18) | copy-start | bytes 27652
  160.7 268.6 %copy-start.25 = (f32[2304]{0:T(1024)S(1)}, f32[2304]{0:T(1024)}, u32[]{:S(2)}) copy-start(f32[2304]{0:T(1024)} %param.17) | copy-start | bytes 27652
  160.7 352.5 %copy-start.1 = (bf16[256,3]{0,1:T(4,128)(2,1)S(1)}, bf16[256,3]{0,1:T(4,128)(2,1)}, u32[]{:S(2)}) copy-start(bf16[256,3]{0,1:T(4,128)(2,1)} %param.15) | copy-start | bytes 4612
Sparse Core Ops, SparseCore 0:
  19.0 108.0 all-gather.2
  160.8 268.3 all-reduce.8
where the time goes:
time: 521 us; the launch traced here: 520 us
  waiting for transfers between devices  350 us (67%)
  blocking collectives  78 us (15%)
  other arithmetic  19.8 us (4%)
  local copies, waits for them, and re-layouts  19.6 us (4%)
  starting transfers between devices  17.8 us (3%)
  between operations  17.3 us (3%)
  matrix products  17.2 us (3%)
    unnamed x3, waiting for transfers between devices  269 us
    all_gather x1, waiting for transfers between devices, body(): lax.all_gather(w_second.astype(jnp.bfloat16), ('tile', 'dp'), axis=0, til...  80.8 us
    psum x1, blocking collectives, body(): lax.psum((jnp.sum(w_first * w_first), jnp.sum(upd_first * upd_first), jnp...  78 us
    ppermute x3, starting transfers between devices, extended(): lax.ppermute(tail, axis, [(i, (i + 1) % count) for i in range(ends)])  13.6 us
    unnamed x55, local copies, waits for them, and re-layouts  12.2 us
  transfers between devices with their start and end apart: 8, of which 3 were waited for; matrix products, arithmetic and copies ran while one was open for 3% of the time, Pallas kernels for 0%

commit v1 on v0

v1 whole, which is shorter than its diff:
```python
import jax
import jax.numpy as jnp
from jax import lax
from jax.experimental import pallas as pl
from jax.experimental.pallas import tpu as pltpu
from jax.sharding import PartitionSpec as P

STEP = 10

beta_one = 0.9
beta_two = 0.999
epsilon = 1e-06
weight_decay = 0.01
learn_rate = 0.002

MESH = pl.DeviceIdType.MESH
BF = jnp.bfloat16
F32 = jnp.float32
NZ, NA = 8, 4
H, WD, CH = 8, 288, 256
PIX = H * WD
GROUPS = ((1, 3, 5), (0, 0, 3), (2, 5, 8))


def dev(z, x, y, c):
    return {"tile": z, "dp": x * 8 + y * 2 + c}


def rcopy(src, dst, ssem, rsem, where):
    return pltpu.make_async_remote_copy(
        src_ref=src,
        dst_ref=dst,
        send_sem=ssem,
        recv_sem=rsem,
        device_id=where,
        device_id_type=MESH,
    )


def loop(lo, hi, fn):
    lax.fori_loop(lo, hi, lambda i, carry: (fn(i), carry)[1], 0)


def kernel(
    x_hbm, p1_hbm, p2_hbm, lab, c3, w1, m1, v1, w2, m2, v2,
    ow1, om1, ov1, ow2, om2, ov2, os1, os2,
    xv, p1, p2, xt, gs, wsend, g0, ga_, wf, wd,
    st, precv, asend, arecv, bsend, brecv, zsend, zrecv, fsend, frecv, gfin, nbuf, nmid,
    ld, s_g0, r_g0, s_g1, r_g1, s_g2, r_g2, s_g3, r_g3, s_h, r_h,
    s_p, r_p, s_a, r_a, s_b, r_b, s_z, r_z, s_f, r_f, s_n, r_n,
):
    z = lax.axis_index("tile")
    d = lax.axis_index("dp")
    x = d // 8
    y = (d // 2) % 4
    c = d % 2
    a = (1 - c) * x + c * y
    b = (1 - c) * y + c * x

    def ab(aa, bb):
        return dev(z, (1 - c) * aa + c * bb, (1 - c) * bb + c * aa, c)

    cp_p2 = pltpu.make_async_copy(p2_hbm, p2, ld.at[0])
    cp_p1 = pltpu.make_async_copy(p1_hbm, p1, ld.at[1])
    cp_x = pltpu.make_async_copy(x_hbm, xv, ld.at[2])
    cp_p2.start()
    cp_p1.start()
    cp_x.start()

    bar = pltpu.get_barrier_semaphore()

    def sig_zc(i):
        k = (z * 2 + c + i) % 16
        pl.semaphore_signal(bar, inc=1, device_id=dev(k // 2, x, y, k % 2), device_id_type=MESH)

    def sig_xy(i):
        k = (x * 4 + y + i) % 16
        pl.semaphore_signal(bar, inc=1, device_id=dev(z, k // 4, k % 4, c), device_id_type=MESH)

    def sig_tr(i):
        pl.semaphore_signal(bar, inc=1, device_id=dev(i // 2, y, x, i % 2), device_id_type=MESH)

    loop(1, 16, sig_zc)
    loop(1, 16, sig_xy)

    @pl.when(x != y)
    def _():
        loop(0, 16, sig_tr)

    for h in (0, 1):
        wsend[h, 0:9, :] = w2[pl.ds(h, 9, stride=2), :].astype(BF)

    @pl.when(x == y)
    def _():
        pl.semaphore_wait(bar, 30)

    @pl.when(x != y)
    def _():
        pl.semaphore_wait(bar, 46)

    slot = z * 2 + c
    own0 = c == 0
    own1 = jnp.logical_and(c == 1, x == y)

    def g0_copy(h, i):
        where = dev((z + i) % NZ, x, y, 0) if h == 0 else dev((z + i) % NZ, y, x, 1)
        return rcopy(wsend.at[h], g0.at[slot], s_g0.at[h, i], r_g0.at[slot], where)

    for h, own in ((0, own0), (1, own1)):
        loop(1, NZ, lambda i, h=h: g0_copy(h, i).start())

        @pl.when(jnp.logical_not(own))
        def _(h=h):
            g0_copy(h, 0).start()

        @pl.when(own)
        def _(h=h):
            g0[slot] = wsend[h]

    own_any = jnp.logical_or(own0, own1)

    def g0_finish():
        def one(s):
            @pl.when(jnp.logical_not(jnp.logical_and(s == slot, own_any)))
            def _():
                rcopy(g0.at[s], g0.at[s], s_g0.at[0, 0], r_g0.at[s], dev(z, x, y, c)).wait_recv()

        loop(0, 16, one)
        pack = jnp.concatenate([g0[s, 0:16, :].astype(F32)[0:9] for s in range(16)], axis=0)
        ga_[a, b] = pack.astype(BF)

        def send(i):
            rcopy(ga_.at[a, b], ga_.at[a, b], s_g1.at[i], r_g1.at[b], ab(a, (b + i) % NA)).start()

        loop(1, NA, send)

    def g1_finish():
        def wait(i):
            k = (b + i) % NA
            rcopy(ga_.at[a, k], ga_.at[a, k], s_g1.at[i], r_g1.at[k], ab(a, k)).wait_recv()

        loop(1, NA, wait)

        def send(i):
            rcopy(ga_.at[a], ga_.at[a], s_g2.at[i], r_g2.at[a], ab((a + i) % NA, b)).start()

        loop(1, NA, send)

    other = dev(z, x, y, 1 - c)

    def g3_copy():
        return rcopy(wd.at[c], wd.at[c], s_g3, r_g3, other)

    def g2_finish():
        def wait(i):
            k = (a + i) % NA
            rcopy(ga_.at[k], ga_.at[k], s_g2.at[i], r_g2.at[k], ab(k, b)).wait_recv()

        loop(1, NA, wait)

        def unpack(aa):
            base = pl.multiple_of(aa * 72, 8)
            for bb in range(NA):
                block = ga_[aa, bb].astype(F32)
                for zz in range(NZ):
                    wf[pl.ds(base + 288 * zz + 18 * bb, 18), :] = block[18 * zz:18 * zz + 18]

        loop(0, NA, unpack)
        wd[c] = wf[...].astype(BF)
        g3_copy().start()

    cols = lax.broadcasted_iota(jnp.int32, (WD, CH), 0)

    def put_row(layer, row, g):
        at = pl.ds(pl.multiple_of(row * WD, 32), WD)
        gs[layer, 1, at, :] = g.astype(BF)
        gs[layer, 0, at, :] = jnp.where(cols == WD - 1, 0.0, pltpu.roll(g, WD - 1, 0)).astype(BF)
        gs[layer, 2, at, :] = jnp.where(cols == 0, 0.0, pltpu.roll(g, 1, 0)).astype(BF)

    def halo_copy(layer, down):
        src = H if down else 1
        dst = 0 if down else H + 1
        k = 1 if down else 0
        where = dev((z + 1) % NZ, x, y, c) if down else dev((z + NZ - 1) % NZ, x, y, c)
        return rcopy(
            gs.at[layer, 1, pl.ds(src * WD, WD)],
            gs.at[layer, 1, pl.ds(dst * WD, WD)],
            s_h.at[layer, k], r_h.at[layer, k], where,
        )

    def halo_start(layer):
        halo_copy(layer, True).start()
        halo_copy(layer, False).start()

    def halo_finish(layer):
        halo_copy(layer, True).wait_recv()
        halo_copy(layer, False).wait_recv()
        for row, edge in ((0, z == 0), (H + 1, z == NZ - 1)):
            g = gs[layer, 1, pl.ds(row * WD, WD), :].astype(F32)
            put_row(layer, row, jnp.where(edge, 0.0, g))

    cls_row = lax.broadcasted_iota(jnp.int32, (8, WD), 0)
    valid = cls_row < 3

    def second_row(r):
        at = pl.ds(pl.multiple_of(r * WD, 32), WD)
        pre = p2[at, :]
        act = jnp.maximum(pre, jnp.zeros_like(pre))
        logits = lax.dot_general(
            c3[0:16, :], act, (((1,), (1,)), ((), ())), preferred_element_type=F32
        )[0:8]
        top = jnp.max(jnp.where(valid, logits, -1e30), axis=0, keepdims=True)
        expo = jnp.where(valid, jnp.exp(logits - top), 0.0)
        prob = expo / jnp.sum(expo, axis=0, keepdims=True)
        onehot = (cls_row == lab[pl.ds(r, 1), :]).astype(F32)
        dlogit = jnp.where(valid, prob - onehot, 0.0)
        high = dlogit.astype(BF).astype(F32)
        rest = dlogit - high
        mid = rest.astype(BF).astype(F32)
        low = rest - mid
        parts = jnp.concatenate([high, mid, low, jnp.zeros_like(low)], axis=0).astype(BF)
        grad = lax.dot_general(
            parts, c3[...], (((0,), (0,)), ((), ())), preferred_element_type=F32
        )
        put_row(0, r + 1, jnp.where(pre.astype(F32) > 0, grad, 0.0))

    def transpose_in(src, relu):
        def one(k):
            at = pl.ds(pl.multiple_of(k * 256, 256), 256)
            block = src[at, :]
            if relu:
                block = jnp.maximum(block, jnp.zeros_like(block))
            xt[:, at] = block.T

        loop(0, PIX // 256, one)

    def pair_copy(layer, group):
        dy = GROUPS[group][0]
        rows = pl.ds(dy * 768, 768)
        return rcopy(
            st.at[layer, 1 - c, rows], precv.at[layer, rows],
            s_p.at[layer, group], r_p.at[layer, group], other,
        )

    def taps(layer, group):
        dy = GROUPS[group][0]

        def one(dx):
            window = gs[layer, dx, pl.ds((2 - dy) * WD, PIX), :]
            part = lax.dot_general(
                xt[...], window, (((1,), (0,)), ((), ())), preferred_element_type=F32
            )
            at = pl.ds(pl.multiple_of((dy * 3 + dx) * 256, 256), 256)
            st[layer, 0, at, :] = part[:, 0:128]
            st[layer, 1, at, :] = part[:, 128:256]

        loop(0, 3, one)
        pair_copy(layer, group).start()

    def a_copy(layer, group, i):
        _, z0, z1 = GROUPS[group]
        k = (a + i) % NA
        return rcopy(
            asend.at[layer, k, pl.ds(z0, z1 - z0)], arecv.at[layer, a, pl.ds(z0, z1 - z0)],
            s_a.at[layer, group, i], r_a.at[layer, group, a], ab(k, b),
        )

    def a_start(layer, group):
        pair_copy(layer, group).wait_recv()
        _, z0, z1 = GROUPS[group]

        def one(zz):
            for aa in range(NA):
                at = pl.ds(pl.multiple_of(zz * 288 + aa * 72, 8), 72)
                asend[layer, aa, zz, 0:72, :] = (st[layer, c, at, :] + precv[layer, at, :]).astype(BF)

        loop(z0, z1, one)
        loop(1, NA, lambda i: a_copy(layer, group, i).start())

    def b_copy(layer, i):
        k = (b + i) % NA
        return rcopy(
            bsend.at[layer, k], brecv.at[layer, b],
            s_b.at[layer, i], r_b.at[layer, b], ab(a, k),
        )

    def a_finish(layer):
        for group in range(3):
            _, z0, z1 = GROUPS[group]

            def wait(i, group=group, z0=z0, z1=z1):
                k = (a + i) % NA
                ref = arecv.at[layer, k, pl.ds(z0, z1 - z0)]
                rcopy(ref, ref, s_a.at[layer, group, i], r_a.at[layer, group, k], ab(k, b)).wait_recv()

            loop(1, NA, wait)

        def one(zz):
            at = pl.ds(pl.multiple_of(zz * 288 + a * 72, 8), 72)
            total = st[layer, c, at, :] + precv[layer, at, :]
            for i in range(1, NA):
                total = total + arecv[layer, (a + i) % NA, zz, 0:72, :].astype(F32)
            for bb in range(NA):
                bsend[layer, bb, zz, 0:18, :] = total[18 * bb:18 * bb + 18]

        loop(0, NZ, one)
        loop(1, NA, lambda i: b_copy(layer, i).start())

    def z_copy(layer, i):
        k = (z + i) % NZ
        return rcopy(
            zsend.at[layer, k], zrecv.at[layer, z],
            s_z.at[layer, i], r_z.at[layer, z], dev(k, x, y, c),
        )

    def b_finish(layer):
        def wait(i):
            k = (b + i) % NA
            rcopy(
                brecv.at[layer, k], brecv.at[layer, k], s_b.at[layer, i], r_b.at[layer, k], ab(a, k)
            ).wait_recv()

        loop(1, NA, wait)

        def one(zz):
            total = bsend[layer, b, zz, 0:18, :]
            for i in range(1, NA):
                total = total + brecv[layer, (b + i) % NA, zz, 0:18, :]
            zsend[layer, zz, 0:18, :] = total

        loop(0, NZ, one)
        loop(1, NZ, lambda i: z_copy(layer, i).start())

    def f_own(cc):
        return own0 if cc == 0 else own1

    def f_copy(layer, cc):
        return rcopy(
            fsend.at[layer, cc], frecv.at[layer, c],
            s_f.at[layer, cc], r_f.at[layer, c], dev(z, a, b, cc),
        )

    def z_finish(layer):
        def wait(i):
            k = (z + i) % NZ
            rcopy(
                zrecv.at[layer, k], zrecv.at[layer, k],
                s_z.at[layer, i], r_z.at[layer, k], dev(k, x, y, c),
            ).wait_recv()

        loop(1, NZ, wait)
        total = zsend[layer, z, 0:18, :]
        for i in range(1, NZ):
            total = total + zrecv[layer, (z + i) % NZ, 0:18, :]
        for cc in range(2):
            fsend[layer, cc, 0:9, :] = total[9 * cc:9 * cc + 9]

            @pl.when(jnp.logical_not(f_own(cc)))
            def _(cc=cc):
                f_copy(layer, cc).start()

            @pl.when(f_own(cc))
            def _(cc=cc):
                frecv[layer, c] = fsend[layer, cc]

    def f_finish(layer):
        for cc in range(2):
            @pl.when(jnp.logical_not(f_own(cc)))
            def _(cc=cc):
                ref = frecv.at[layer, cc]
                rcopy(ref, ref, s_f.at[layer, cc], r_f.at[layer, cc], dev(z, a, b, cc)).wait_recv()

            gfin[layer, pl.ds(cc, 9, stride=2), :] = frecv[layer, cc, 0:9, :]
        return gfin[layer]

    def moments(grad, weight, first, second):
        first_new = beta_one * first + (1.0 - beta_one) * grad
        second_new = beta_two * second + (1.0 - beta_two) * grad * grad
        corr_one = 1.0 - beta_one**STEP
        corr_two = 1.0 - beta_two**STEP
        update = (
            first_new / corr_one / (jnp.sqrt(second_new / corr_two) + epsilon)
            + weight_decay * weight
        )
        return (first_new, second_new, update)

    def first_row(r):
        total = jnp.zeros((WD, CH), F32)
        for dy in range(3):
            at = pl.ds(pl.multiple_of((r + 2 - dy) * WD, 32), WD)
            for dx in range(3):
                t = (dy * 3 + dx) * 256
                tap = jnp.concatenate([wd[0, t:t + 256, :], wd[1, t:t + 256, :]], axis=1)
                total = total + lax.dot_general(
                    gs[0, dx, at, :], tap, (((1,), (1,)), ((), ())), preferred_element_type=F32
                )
        pre = p1[pl.ds(pl.multiple_of(r * WD, 32), WD), :]
        put_row(1, r + 1, jnp.where(pre.astype(F32) > 0, total, 0.0))

    cp_p2.wait()
    loop(0, 2, lambda i: second_row(i * (H - 1)))
    halo_start(0)
    g0_finish()
    loop(1, H - 1, second_row)
    g1_finish()
    cp_p1.wait()
    transpose_in(p1, True)
    taps(0, 0)
    g2_finish()
    halo_finish(0)
    taps(0, 1)
    a_start(0, 0)
    taps(0, 2)
    a_start(0, 1)
    cp_x.wait()
    transpose_in(xv, False)
    a_start(0, 2)
    g3_copy().wait_recv()
    loop(0, 2, lambda i: first_row(i * (H - 1)))
    halo_start(1)
    loop(1, H - 1, first_row)
    a_finish(0)
    taps(1, 0)
    b_finish(0)
    halo_finish(1)
    taps(1, 1)
    a_start(1, 0)
    z_finish(0)
    taps(1, 2)
    a_start(1, 1)
    m2n, v2n, u2 = moments(f_finish(0), w2[...], m2[...], v2[...])
    om2[...] = m2n
    ov2[...] = v2n
    os2[...] = u2
    a_start(1, 2)
    a_finish(1)
    b_finish(1)
    z_finish(1)
    m1n, v1n, u1 = moments(f_finish(1), w1[...], m1[...], v1[...])
    om1[...] = m1n
    ov1[...] = v1n

    def squares(value):
        return jnp.sum(value * value, axis=0, keepdims=True)

    u2 = os2[...]
    nbuf[0, slot] = jnp.concatenate(
        [squares(w1[...]), squares(u1), squares(w2[...]), squares(u2), jnp.zeros((4, 128), F32)],
        axis=0,
    )
    place = x * 4 + y

    def n_copy(stage, i):
        if stage == 0:
            k = (slot + i) % 16
            return rcopy(
                nbuf.at[0, slot], nbuf.at[0, slot], s_n.at[0, i], r_n.at[0, slot],
                dev(k // 2, x, y, k % 2),
            )
        k = (place + i) % 16
        return rcopy(
            nbuf.at[1, place], nbuf.at[1, place], s_n.at[1, i], r_n.at[1, place],
            dev(z, k // 4, k % 4, c),
        )

    def n_wait(stage, i):
        k = ((slot if stage == 0 else place) + i) % 16
        ref = nbuf.at[stage, k]
        rcopy(ref, ref, s_n.at[stage, i], r_n.at[stage, k], other).wait_recv()

    loop(1, 16, lambda i: n_copy(0, i).start())
    loop(1, 16, lambda i: n_wait(0, i))
    nbuf[1, place] = jnp.sum(nbuf[0], axis=0)
    loop(1, 16, lambda i: n_copy(1, i).start())
    loop(1, 16, lambda i: n_wait(1, i))
    sums = jnp.sqrt(jnp.sum(jnp.sum(nbuf[1], axis=0), axis=1, keepdims=True))
    step1 = sums[0:1] / sums[1:2] * u1
    step2 = sums[2:3] / sums[3:4] * u2
    os1[...] = step1
    os2[...] = step2
    ow1[...] = w1[...] - learn_rate * step1
    ow2[...] = w2[...] - learn_rate * step2

    for h, own in ((0, own0), (1, own1)):
        loop(1, NZ, lambda i, h=h: g0_copy(h, i).wait_send())

        @pl.when(jnp.logical_not(own))
        def _(h=h):
            g0_copy(h, 0).wait_send()

    def done(i):
        rcopy(ga_.at[a, b], ga_.at[a, b], s_g1.at[i], r_g1.at[b], other).wait_send()
        rcopy(ga_.at[a], ga_.at[a], s_g2.at[i], r_g2.at[a], other).wait_send()
        for layer in range(2):
            for group in range(3):
                a_copy(layer, group, i).wait_send()
            b_copy(layer, i).wait_send()

    loop(1, NA, done)
    g3_copy().wait_send()
    for layer in range(2):
        halo_copy(layer, True).wait_send()
        halo_copy(layer, False).wait_send()
        for group in range(3):
            pair_copy(layer, group).wait_send()
        loop(1, NZ, lambda i, layer=layer: z_copy(layer, i).wait_send())
        for cc in range(2):
            @pl.when(jnp.logical_not(f_own(cc)))
            def _(cc=cc, layer=layer):
                f_copy(layer, cc).wait_send()

    for stage in range(2):
        loop(1, 16, lambda i, stage=stage: n_copy(stage, i).wait_send())


def body(
    inputs, pre_first, pre_second, labels, classifier,
    w_first, m_first, v_first, w_second, m_second, v_second,
):
    flat = [t.reshape(18, 128) for t in (w_first, m_first, v_first, w_second, m_second, v_second)]
    c3 = jnp.tile(jnp.pad(classifier.T, ((0, 5), (0, 0))), (4, 1))
    vm = pl.BlockSpec(memory_space=pltpu.VMEM)
    hb = pl.BlockSpec(memory_space=pl.ANY)
    dma = pltpu.SemaphoreType.DMA
    outs = pl.pallas_call(
        kernel,
        out_shape=[jax.ShapeDtypeStruct((18, 128), F32)] * 8,
        in_specs=[hb] * 3 + [vm] * 8,
        out_specs=[vm] * 8,
        scratch_shapes=[
            pltpu.VMEM((PIX, CH), BF),
            pltpu.VMEM((PIX, CH), BF),
            pltpu.VMEM((PIX, CH), BF),
            pltpu.VMEM((CH, PIX), BF),
            pltpu.VMEM((2, 3, (H + 2) * WD, CH), BF),
            pltpu.VMEM((2, 16, 128), BF),
            pltpu.VMEM((16, 16, 128), BF),
            pltpu.VMEM((NA, NA, 144, 128), BF),
            pltpu.VMEM((2304, 128), F32),
            pltpu.VMEM((2, 2304, 128), BF),
            pltpu.VMEM((2, 2, 2304, 128), F32),
            pltpu.VMEM((2, 2304, 128), F32),
            pltpu.VMEM((2, NA, NZ, 80, 128), BF),
            pltpu.VMEM((2, NA, NZ, 80, 128), BF),
            pltpu.VMEM((2, NA, NZ, 24, 128), F32),
            pltpu.VMEM((2, NA, NZ, 24, 128), F32),
            pltpu.VMEM((2, NZ, 24, 128), F32),
            pltpu.VMEM((2, NZ, 24, 128), F32),
            pltpu.VMEM((2, 2, 16, 128), F32),
            pltpu.VMEM((2, 2, 16, 128), F32),
            pltpu.VMEM((2, 18, 128), F32),
            pltpu.VMEM((2, 16, 8, 128), F32),
            pltpu.VMEM((8, 128), F32),
            dma((3,)),
            dma((2, NZ)), dma((16,)),
            dma((NA,)), dma((NA,)),
            dma((NA,)), dma((NA,)),
            dma, dma,
            dma((2, 2)), dma((2, 2)),
            dma((2, 3)), dma((2, 3)),
            dma((2, 3, NA)), dma((2, 3, NA)),
            dma((2, NA)), dma((2, NA)),
            dma((2, NZ)), dma((2, NZ)),
            dma((2, 2)), dma((2, 2)),
            dma((2, 16)), dma((2, 16)),
        ],
        compiler_params=pltpu.CompilerParams(
            collective_id=0, has_side_effects=True, vmem_limit_bytes=56 * 1024 * 1024
        ),
        cost_estimate=pl.CostEstimate(
            flops=2 * 27 * PIX * CH * CH, bytes_accessed=4_000_000, transcendentals=3 * PIX
        ),
    )(
        inputs.reshape(PIX, CH), pre_first.reshape(PIX, CH), pre_second.reshape(PIX, CH),
        labels[0], c3, *flat,
    )
    return tuple(t.reshape(2304) for t in outs)


def solution(mesh):
    grid = P("dp", "tile", None, None)
    flat = P(("tile", "dp"))
    return jax.shard_map(
        body,
        mesh=mesh,
        in_specs=(grid, grid, grid, P("dp", "tile", None), P(), flat, flat, flat, flat, flat, flat),
        out_specs=(flat,) * 8,
        check_vma=False,
    )
```

time: 521 us -> 96.6 us (0.19)
  waiting for transfers between devices: 350 us -> 0 us
  Pallas kernels: 0 us -> 83.3 us
  blocking collectives: 78 us -> 0 us
  other arithmetic: 19.8 us -> 0 us
  starting transfers between devices: 17.8 us -> 0 us
  matrix products: 17.2 us -> 0 us
  between operations: 17.3 us -> 0.65 us
  local copies, waits for them, and re-layouts: 19.6 us -> 11.7 us
    unnamed x3 -> x0, waiting for transfers between devices: 269 us -> none
    pallas_call x0 -> x1, Pallas kernels: none -> 83.3 us  [body(): pl.pallas_call(kernel, out_shape=[jax.ShapeDtypeStruct((18, 128), F32)] *...]
    all_gather x1 -> x0, waiting for transfers between devices: 80.8 us -> none  [body(): lax.all_gather(w_second.astype(jnp.bfloat16), ('tile', 'dp'), axis=0, til...]
    psum x1 -> x0, blocking collectives: 78 us -> none  [body(): lax.psum((jnp.sum(w_first * w_first), jnp.sum(upd_first * upd_first), jnp...]
    ppermute x6 -> x0, starting transfers between devices: 17.8 us -> none  [the longest x3 13.6 us: extended(): lax.ppermute(tail, axis, [(i, (i + 1) % count) for i in range(ends)])]
    dot_general x29 -> x0, matrix products: 17.2 us -> none  [the longest x18 9.59 us: weight_terms(): lax.dot_general(window, flat_grad, (((0,), (0,)), ((), ())), preferred_el...]
    all_gather x1 -> x0, other arithmetic: 9.42 us -> none  [body(): lax.all_gather(w_second.astype(jnp.bfloat16), ('tile', 'dp'), axis=0, til...]
    unnamed x55 -> x8, local copies, waits for them, and re-layouts: 12.2 us -> 10.5 us
  transfers between devices with their start and end apart: 8 -> 0, of which waited for: 3 -> 0; matrix products, arithmetic and copies ran while one was open for 3% -> 0% of each run, Pallas kernels for 0% -> 0%
where the time goes in v1:
time: 96.6 us; the launch traced here: 95.7 us
  Pallas kernels  83.3 us (86%)
  local copies, waits for them, and re-layouts  11.7 us (12%)
    pallas_call x1, Pallas kernels, body(): pl.pallas_call(kernel, out_shape=[jax.ShapeDtypeStruct((18, 128), F32)] *...  83.3 us
    unnamed x8, local copies, waits for them, and re-layouts  10.5 us

profile of v1, /device:TPU:1, one launch (start us, length us, event | category | flops | bytes accessed | tf_op | source)
XLA Modules:
  0.0 95.7 jit_solution(4345079710705619715)
XLA Ops:
  0.6 0.7 pad.4
  1.3 0.6 broadcast_bitcast_fusion.c3
  1.9 83.3 %shard_map.170 = (f32[18,128]{1,0:T(8,128)}, f32[18,128]{1,0:T(8,128)}, f32[18,128]{1,0:T(8,128)}, f32[18,128]{1,0:T(8,128)}, f32[18,128]{1,0:T(8,128)}, /*index...) custom-call(bf16[2304,256]{1,0:T(8,128)(2,1)} %bitcast.30, bf16[2304,256]{1,0:T(8,128)(2,1)} %bitcast.31, ...), custom_call_target="tpu_custom_call" | custom-call | flops 8153726976 | bytes 4000000 | tf_op jit(solution)/shard_map/pallas_call | solution.py:525
  85.2 1.3 %copy.27 = f32[2304]{0:T(1024)} copy(f32[2304]{0:T(1024)} %bitcast.28) | data formatting | bytes 18432
  86.5 1.3 %copy.28 = f32[2304]{0:T(1024)} copy(f32[2304]{0:T(1024)} %bitcast.27) | data formatting | bytes 18432
  87.8 1.3 %copy.29 = f32[2304]{0:T(1024)} copy(f32[2304]{0:T(1024)} %bitcast.26) | data formatting | bytes 18432
  89.2 1.3 %copy.30 = f32[2304]{0:T(1024)} copy(f32[2304]{0:T(1024)} %bitcast.25) | data formatting | bytes 18432
  90.5 1.3 %copy.31 = f32[2304]{0:T(1024)} copy(f32[2304]{0:T(1024)} %bitcast.24) | data formatting | bytes 18432
  91.8 1.3 %copy.32 = f32[2304]{0:T(1024)} copy(f32[2304]{0:T(1024)} %bitcast.23) | data formatting | bytes 18432
  93.1 1.3 %copy.33 = f32[2304]{0:T(1024)} copy(f32[2304]{0:T(1024)} %bitcast.22) | data formatting | bytes 18432
  94.4 1.3 %copy.34 = f32[2304]{0:T(1024)} copy(f32[2304]{0:T(1024)} %bitcast.21) | data formatting | bytes 18432

commit v2 on v1

v2 whole, which is shorter than its diff:
```python
import jax
import jax.numpy as jnp
from jax import lax
from jax.experimental import pallas as pl
from jax.experimental.pallas import tpu as pltpu
from jax.sharding import PartitionSpec as P

STEP = 10

beta_one = 0.9
beta_two = 0.999
epsilon = 1e-06
weight_decay = 0.01
learn_rate = 0.002

MESH = pl.DeviceIdType.MESH
BF = jnp.bfloat16
F32 = jnp.float32
NZ, NA = 8, 4
H, WD, CH = 8, 288, 256
PIX = H * WD
GROUPS = (1, 0, 2)
PARTS = (((0, 1), (3, 4, 0, 1, 2), 0, 1440), ((2,), (5, 6, 7), 1440, 2304))


def dev(z, x, y, c):
    return {"tile": z, "dp": x * 8 + y * 2 + c}


def rcopy(src, dst, ssem, rsem, where):
    return pltpu.make_async_remote_copy(
        src_ref=src,
        dst_ref=dst,
        send_sem=ssem,
        recv_sem=rsem,
        device_id=where,
        device_id_type=MESH,
    )


def loop(lo, hi, fn):
    lax.fori_loop(lo, hi, lambda i, carry: (fn(i), carry)[1], 0)


def kernel(
    x_hbm, p1_hbm, p2_hbm, lab, ct, w1, m1, v1, w2, m2, v2,
    outs,
    xv, p1, p2, xt, gs, c3, wsend, g0, ga_, wf, wd,
    st, precv, tot, asend0, arecv0, asend1, arecv1, zsend, zrecv, gfin, nbuf,
    ld, s_g0, r_g0, s_g1, r_g1, s_g2, r_g2, s_g3, r_g3, s_h, r_h,
    s_p, r_p, s_a, r_a, s_z, r_z, s_n, r_n,
):
    z = lax.axis_index("tile")
    d = lax.axis_index("dp")
    x = d // 8
    y = (d // 2) % 4
    c = d % 2
    a = (1 - c) * x + c * y
    b = (1 - c) * y + c * x

    def ab(aa, bb):
        return dev(z, (1 - c) * aa + c * bb, (1 - c) * bb + c * aa, c)

    cp_p2 = pltpu.make_async_copy(p2_hbm, p2, ld.at[0])
    cp_p1 = pltpu.make_async_copy(p1_hbm, p1, ld.at[1])
    cp_x = pltpu.make_async_copy(x_hbm, xv, ld.at[2])
    cp_p2.start()
    cp_p1.start()
    cp_x.start()

    bar = pltpu.get_barrier_semaphore()

    def sig_zc(i):
        k = (z * 2 + c + i) % 16
        pl.semaphore_signal(bar, inc=1, device_id=dev(k // 2, x, y, k % 2), device_id_type=MESH)

    def sig_xy(i):
        k = (x * 4 + y + i) % 16
        pl.semaphore_signal(bar, inc=1, device_id=dev(z, k // 4, k % 4, c), device_id_type=MESH)

    loop(1, 16, sig_zc)
    loop(1, 16, sig_xy)

    for h in (0, 1):
        wsend[h, 0:9, :] = w2[pl.ds(h, 9, stride=2), :].astype(BF)

    table = jnp.concatenate([ct[...].astype(F32), jnp.zeros((5, CH), F32)], axis=0)
    c3[...] = jnp.concatenate([table] * 4, axis=0).astype(BF)

    slot = z * 2 + c
    place = x * 4 + y

    def g0_copy(i):
        k = (slot + i) % 16
        return rcopy(
            wsend.at[k % 2], g0.at[slot], s_g0.at[i], r_g0.at[slot], dev(k // 2, x, y, k % 2)
        )

    def g0_start():
        g0[slot] = wsend[c]
        loop(1, 16, lambda i: g0_copy(i).start())

    def g1_copy(i):
        return rcopy(
            ga_.at[a, b], ga_.at[a, b], s_g1.at[i], r_g1.at[b], ab(a, (b + i) % NA)
        )

    def g2_copy(k, i):
        return rcopy(
            ga_.at[a, k], ga_.at[a, k], s_g2.at[k, i], r_g2.at[a, k], ab((a + i) % NA, b)
        )

    def g0_finish():
        def one(i):
            k = (slot + i) % 16
            rcopy(g0.at[k], g0.at[k], s_g0.at[i], r_g0.at[k], dev(z, x, y, c)).wait_recv()

        loop(1, 16, one)
        pack = jnp.concatenate([g0[s, 0:16, :].astype(F32)[0:9] for s in range(16)], axis=0)
        ga_[a, b] = pack.astype(BF)
        loop(1, NA, lambda i: g1_copy(i).start())
        loop(1, NA, lambda i: g2_copy(b, i).start())

    def g1_finish():
        for j in (1, 3, 2):
            k = (b + j) % NA
            rcopy(ga_.at[a, k], ga_.at[a, k], s_g1.at[j], r_g1.at[k], ab(a, k)).wait_recv()
            loop(1, NA, lambda i, k=k: g2_copy(k, i).start())

    other = dev(z, x, y, 1 - c)

    def g3_copy():
        return rcopy(wd.at[c], wd.at[c], s_g3, r_g3, other)

    def g2_finish():
        def wait(i):
            k = (a + i) % NA
            for j in range(NA):
                rcopy(
                    ga_.at[k, j], ga_.at[k, j], s_g2.at[j, i], r_g2.at[k, j], ab(k, b)
                ).wait_recv()

        loop(1, NA, wait)

        def unpack(xx):
            base = pl.multiple_of(xx * 72, 8)
            for yy in range(NA):
                block = ga_[(1 - c) * xx + c * yy, (1 - c) * yy + c * xx].astype(F32)
                for zz in range(NZ):
                    wf[pl.ds(base + 288 * zz + 18 * yy, 18), :] = block[18 * zz:18 * zz + 18]

        loop(0, NA, unpack)
        wd[c] = wf[...].astype(BF)
        g3_copy().start()

    cols = lax.broadcasted_iota(jnp.int32, (WD, CH), 0)

    def put_row(layer, row, g):
        at = pl.ds(pl.multiple_of(row * WD, 32), WD)
        gs[layer, 1, at, :] = g.astype(BF)
        gs[layer, 0, at, :] = jnp.where(cols == WD - 1, 0.0, pltpu.roll(g, WD - 1, 0)).astype(BF)
        gs[layer, 2, at, :] = jnp.where(cols == 0, 0.0, pltpu.roll(g, 1, 0)).astype(BF)

    def halo_copy(layer, down):
        src = H if down else 1
        dst = 0 if down else H + 1
        k = 1 if down else 0
        where = dev((z + 1) % NZ, x, y, c) if down else dev((z + NZ - 1) % NZ, x, y, c)
        return rcopy(
            gs.at[layer, 1, pl.ds(src * WD, WD)],
            gs.at[layer, 1, pl.ds(dst * WD, WD)],
            s_h.at[layer, k], r_h.at[layer, k], where,
        )

    def halo_start(layer):
        halo_copy(layer, True).start()
        halo_copy(layer, False).start()

    def halo_finish(layer):
        halo_copy(layer, True).wait_recv()
        halo_copy(layer, False).wait_recv()
        for row, edge in ((0, z == 0), (H + 1, z == NZ - 1)):
            g = gs[layer, 1, pl.ds(row * WD, WD), :].astype(F32)
            put_row(layer, row, jnp.where(edge, 0.0, g))

    cls_row = lax.broadcasted_iota(jnp.int32, (8, WD), 0)
    valid = cls_row < 3

    def second_row(r):
        at = pl.ds(pl.multiple_of(r * WD, 32), WD)
        pre = p2[at, :]
        act = jnp.maximum(pre, jnp.zeros_like(pre))
        logits = lax.dot_general(
            c3[0:16, :], act, (((1,), (1,)), ((), ())), preferred_element_type=F32
        )[0:8]
        top = jnp.max(jnp.where(valid, logits, -1e30), axis=0, keepdims=True)
        expo = jnp.where(valid, jnp.exp(logits - top), 0.0)
        prob = expo / jnp.sum(expo, axis=0, keepdims=True)
        onehot = (cls_row == lab[pl.ds(r, 1), :]).astype(F32)
        dlogit = jnp.where(valid, prob - onehot, 0.0)
        high = dlogit.astype(BF).astype(F32)
        rest = dlogit - high
        mid = rest.astype(BF).astype(F32)
        low = rest - mid
        parts = jnp.concatenate([high, mid, low, jnp.zeros_like(low)], axis=0).astype(BF)
        grad = lax.dot_general(
            parts, c3[...], (((0,), (0,)), ((), ())), preferred_element_type=F32
        )
        put_row(0, r + 1, jnp.where(pre.astype(F32) > 0, grad, 0.0))

    def transpose_in(src, relu):
        def one(k):
            at = pl.ds(pl.multiple_of(k * 256, 256), 256)
            block = src[at, :]
            if relu:
                block = jnp.maximum(block, jnp.zeros_like(block))
            xt[:, at] = block.T

        loop(0, PIX // 256, one)

    def pair_copy(layer, group):
        dy = GROUPS[group]
        rows = pl.ds(dy * 768, 768)
        return rcopy(
            st.at[layer, 1 - c, rows], precv.at[layer, rows],
            s_p.at[layer, group], r_p.at[layer, group], other,
        )

    def taps(layer, group):
        dy = GROUPS[group]

        def one(dx):
            window = gs[layer, dx, pl.ds((2 - dy) * WD, PIX), :]
            part = lax.dot_general(
                xt[...], window, (((1,), (0,)), ((), ())), preferred_element_type=F32
            )
            at = pl.ds(pl.multiple_of((dy * 3 + dx) * 256, 256), 256)
            st[layer, 0, at, :] = part[:, 0:128]
            st[layer, 1, at, :] = part[:, 128:256]

        loop(0, 3, one)
        pair_copy(layer, group).start()

    def pack_refs(part):
        return (asend0, arecv0) if part == 0 else (asend1, arecv1)

    def a_copy(layer, part, i):
        send, recv = pack_refs(part)
        k = (place + i) % 16
        return rcopy(
            send.at[layer, k], recv.at[layer, place],
            s_a.at[layer, part, i], r_a.at[layer, part, place], dev(z, k // 4, k % 4, c),
        )

    def a_start(layer, part):
        for group in PARTS[part][0]:
            pair_copy(layer, group).wait_recv()
        _, zs, lo, hi = PARTS[part]
        tot[lo:hi, :] = st[layer, c, lo:hi, :] + precv[layer, lo:hi, :]
        send = pack_refs(part)[0]
        rows = 18 * len(zs)

        def one(xx):
            base = pl.multiple_of(xx * 72, 8)
            for yy in range(NA):
                block = jnp.concatenate(
                    [tot[pl.ds(base + 288 * zz + 18 * yy, 18), :] for zz in zs]
                    + [jnp.zeros((send.shape[2] - rows, 128), F32)],
                    axis=0,
                )
                send[layer, xx * 4 + yy] = block.astype(BF)

        loop(0, NA, one)
        loop(1, 16, lambda i: a_copy(layer, part, i).start())

    def z_copy(layer, i):
        k = (slot + i) % 16
        return rcopy(
            zsend.at[layer, k], zrecv.at[layer, slot],
            s_z.at[layer, i], r_z.at[layer, slot], dev(k // 2, x, y, k % 2),
        )

    def a_finish(layer):
        for part in range(2):
            send, recv = pack_refs(part)

            def wait(i, part=part, recv=recv):
                k = (place + i) % 16
                rcopy(
                    recv.at[layer, k], recv.at[layer, k],
                    s_a.at[layer, part, i], r_a.at[layer, part, k], other,
                ).wait_recv()

            loop(1, 16, wait)
            total = lax.fori_loop(
                1, 16,
                lambda i, acc, recv=recv: acc + recv[layer, (place + i) % 16].astype(F32),
                send[layer, place].astype(F32),
            )
            for j, zz in enumerate(PARTS[part][1]):
                for cc in range(2):
                    r = 18 * j + 9 * cc
                    zsend[layer, 2 * zz + cc, 0:9, :] = total[r:r + 9]

        zrecv[layer, slot] = zsend[layer, slot]
        loop(1, 16, lambda i: z_copy(layer, i).start())

    def z_finish(layer):
        def wait(i):
            k = (slot + i) % 16
            rcopy(
                zrecv.at[layer, k], zrecv.at[layer, k],
                s_z.at[layer, i], r_z.at[layer, k], other,
            ).wait_recv()

        loop(1, 16, wait)
        for cc in range(2):
            total = zrecv[layer, cc, 0:9, :]
            for zz in range(1, NZ):
                total = total + zrecv[layer, 2 * zz + cc, 0:9, :]
            gfin[layer, pl.ds(cc, 9, stride=2), :] = total
        return gfin[layer]

    def moments(grad, weight, first, second):
        first_new = beta_one * first + (1.0 - beta_one) * grad
        second_new = beta_two * second + (1.0 - beta_two) * grad * grad
        corr_one = 1.0 - beta_one**STEP
        corr_two = 1.0 - beta_two**STEP
        update = (
            first_new / corr_one / (jnp.sqrt(second_new / corr_two) + epsilon)
            + weight_decay * weight
        )
        return (first_new, second_new, update)

    def first_row(r):
        total = jnp.zeros((WD, CH), F32)
        for dy in range(3):
            at = pl.ds(pl.multiple_of((r + 2 - dy) * WD, 32), WD)
            for dx in range(3):
                t = (dy * 3 + dx) * 256
                tap = jnp.concatenate([wd[0, t:t + 256, :], wd[1, t:t + 256, :]], axis=1)
                total = total + lax.dot_general(
                    gs[0, dx, at, :], tap, (((1,), (1,)), ((), ())), preferred_element_type=F32
                )
        pre = p1[pl.ds(pl.multiple_of(r * WD, 32), WD), :]
        put_row(1, r + 1, jnp.where(pre.astype(F32) > 0, total, 0.0))

    cp_p2.wait()
    loop(0, 2, lambda i: second_row(i * (H - 1)))
    pl.semaphore_wait(bar, 30)
    g0_start()
    halo_start(0)
    loop(1, H - 1, second_row)
    g0_finish()
    cp_p1.wait()
    transpose_in(p1, True)
    taps(0, 0)
    g1_finish()
    halo_finish(0)
    taps(0, 1)
    taps(0, 2)
    cp_x.wait()
    transpose_in(xv, False)
    g2_finish()
    a_start(0, 0)
    a_start(0, 1)
    g3_copy().wait_recv()
    loop(0, 2, lambda i: first_row(i * (H - 1)))
    halo_start(1)
    loop(1, H - 1, first_row)
    taps(1, 0)
    halo_finish(1)
    taps(1, 1)
    a_start(1, 0)
    taps(1, 2)
    a_start(1, 1)
    a_finish(0)
    a_finish(1)
    m2n, v2n, u2 = moments(z_finish(0), w2[...], m2[...], v2[...])
    outs[4, 0:18, :] = m2n
    outs[5, 0:18, :] = v2n
    outs[7, 0:18, :] = u2
    m1n, v1n, u1 = moments(z_finish(1), w1[...], m1[...], v1[...])
    outs[1, 0:18, :] = m1n
    outs[2, 0:18, :] = v1n

    def squares(value):
        return jnp.sum(value * value, axis=0, keepdims=True)

    u2 = outs[7, 0:18, :]
    nbuf[0, slot] = jnp.concatenate(
        [squares(w1[...]), squares(u1), squares(w2[...]), squares(u2), jnp.zeros((4, 128), F32)],
        axis=0,
    )
    def n_copy(stage, i):
        if stage == 0:
            k = (slot + i) % 16
            return rcopy(
                nbuf.at[0, slot], nbuf.at[0, slot], s_n.at[0, i], r_n.at[0, slot],
                dev(k // 2, x, y, k % 2),
            )
        k = (place + i) % 16
        return rcopy(
            nbuf.at[1, place], nbuf.at[1, place], s_n.at[1, i], r_n.at[1, place],
            dev(z, k // 4, k % 4, c),
        )

    def n_wait(stage, i):
        k = ((slot if stage == 0 else place) + i) % 16
        ref = nbuf.at[stage, k]
        rcopy(ref, ref, s_n.at[stage, i], r_n.at[stage, k], other).wait_recv()

    loop(1, 16, lambda i: n_copy(0, i).start())
    loop(1, 16, lambda i: n_wait(0, i))
    nbuf[1, place] = jnp.sum(nbuf[0], axis=0)
    loop(1, 16, lambda i: n_copy(1, i).start())
    loop(1, 16, lambda i: n_wait(1, i))
    sums = jnp.sqrt(jnp.sum(jnp.sum(nbuf[1], axis=0), axis=1, keepdims=True))
    step1 = sums[0:1] / sums[1:2] * u1
    step2 = sums[2:3] / sums[3:4] * u2
    outs[6, 0:18, :] = step1
    outs[7, 0:18, :] = step2
    outs[0, 0:18, :] = w1[...] - learn_rate * step1
    outs[3, 0:18, :] = w2[...] - learn_rate * step2

    def done(i):
        g0_copy(i).wait_send()
        for layer in range(2):
            for part in range(2):
                a_copy(layer, part, i).wait_send()
            z_copy(layer, i).wait_send()
        for stage in range(2):
            n_copy(stage, i).wait_send()

    loop(1, 16, done)

    def done_gather(i):
        g1_copy(i).wait_send()
        for k in range(NA):
            g2_copy(k, i).wait_send()

    loop(1, NA, done_gather)
    g3_copy().wait_send()
    for layer in range(2):
        halo_copy(layer, True).wait_send()
        halo_copy(layer, False).wait_send()
        for group in range(3):
            pair_copy(layer, group).wait_send()


def body(
    inputs, pre_first, pre_second, labels, classifier,
    w_first, m_first, v_first, w_second, m_second, v_second,
):
    flat = [t.reshape(18, 128) for t in (w_first, m_first, v_first, w_second, m_second, v_second)]
    vm = pl.BlockSpec(memory_space=pltpu.VMEM)
    hb = pl.BlockSpec(memory_space=pl.ANY)
    dma = pltpu.SemaphoreType.DMA
    outs = pl.pallas_call(
        kernel,
        out_shape=jax.ShapeDtypeStruct((8, 24, 128), F32),
        in_specs=[hb] * 3 + [vm] * 8,
        out_specs=vm,
        scratch_shapes=[
            pltpu.VMEM((PIX, CH), BF),
            pltpu.VMEM((PIX, CH), BF),
            pltpu.VMEM((PIX, CH), BF),
            pltpu.VMEM((CH, PIX), BF),
            pltpu.VMEM((2, 3, (H + 2) * WD, CH), BF),
            pltpu.VMEM((32, CH), BF),
            pltpu.VMEM((2, 16, 128), BF),
            pltpu.VMEM((16, 16, 128), BF),
            pltpu.VMEM((NA, NA, 144, 128), BF),
            pltpu.VMEM((2304, 128), F32),
            pltpu.VMEM((2, 2304, 128), BF),
            pltpu.VMEM((2, 2, 2304, 128), F32),
            pltpu.VMEM((2, 2304, 128), F32),
            pltpu.VMEM((2304, 128), F32),
            pltpu.VMEM((2, 16, 96, 128), BF),
            pltpu.VMEM((2, 16, 96, 128), BF),
            pltpu.VMEM((2, 16, 64, 128), BF),
            pltpu.VMEM((2, 16, 64, 128), BF),
            pltpu.VMEM((2, 16, 16, 128), F32),
            pltpu.VMEM((2, 16, 16, 128), F32),
            pltpu.VMEM((2, 18, 128), F32),
            pltpu.VMEM((2, 16, 8, 128), F32),
            dma((3,)),
            dma((16,)), dma((16,)),
            dma((NA,)), dma((NA,)),
            dma((NA, NA)), dma((NA, NA)),
            dma, dma,
            dma((2, 2)), dma((2, 2)),
            dma((2, 3)), dma((2, 3)),
            dma((2, 2, 16)), dma((2, 2, 16)),
            dma((2, 16)), dma((2, 16)),
            dma((2, 16)), dma((2, 16)),
        ],
        compiler_params=pltpu.CompilerParams(
            collective_id=0, has_side_effects=True, vmem_limit_bytes=56 * 1024 * 1024
        ),
        cost_estimate=pl.CostEstimate(
            flops=2 * 27 * PIX * CH * CH, bytes_accessed=4_000_000, transcendentals=3 * PIX
        ),
    )(
        inputs.reshape(PIX, CH), pre_first.reshape(PIX, CH), pre_second.reshape(PIX, CH),
        labels[0], classifier.T, *flat,
    )
    return tuple(outs[i, 0:18].reshape(2304) for i in range(8))


def solution(mesh):
    grid = P("dp", "tile", None, None)
    flat = P(("tile", "dp"))
    return jax.shard_map(
        body,
        mesh=mesh,
        in_specs=(grid, grid, grid, P("dp", "tile", None), P(), flat, flat, flat, flat, flat, flat),
        out_specs=(flat,) * 8,
        check_vma=False,
    )
```

time: 96.6 us -> 70.7 us (0.73)
  Pallas kernels: 83.3 us -> 68.4 us
  local copies, waits for them, and re-layouts: 11.7 us -> 1.46 us
    pallas_call x1, Pallas kernels: 83.3 us -> 68.4 us  [body(): pl.pallas_call(kernel, out_shape=jax.ShapeDtypeStruct((8, 24, 128), F32),...]
    unnamed x8 -> x0, local copies, waits for them, and re-layouts: 10.5 us -> none
where the time goes in v2:
time: 70.7 us; the launch traced here: 70.5 us
  Pallas kernels  68.4 us (97%)
  local copies, waits for them, and re-layouts  1.46 us (2%)
    pallas_call x1, Pallas kernels, body(): pl.pallas_call(kernel, out_shape=jax.ShapeDtypeStruct((8, 24, 128), F32),...  68.4 us
    another operation x1, local copies, waits for them, and re-layouts, body(): return tuple((outs[i, 0:18].reshape(2304) for i in range(8)))  1.46 us

profile of v2, /device:TPU:1, one launch (start us, length us, event | category | flops | bytes accessed | tf_op | source)
XLA Modules:
  0.0 70.5 jit_solution(3562720303359800244)
XLA Ops:
  0.6 68.4 %shard_map.170 = f32[8,24,128]{2,1,0:T(8,128)} custom-call(bf16[2304,256]{1,0:T(8,128)(2,1)} %bitcast.27, bf16[2304,256]{1,0:T(8,128)(2,1)} %bitcast.28, bf16[2304,256]{1,0:T(8,128)(2,1)} %bitcast.29, s32[8,288]{1,0:T(8,128)} %bitcast.30, bf16[3,256]{1,0:T(4,128)(2,1)} %bitcast.37, f32[18,128]{1,0:T(8,128)} %bitcast.31, f32[18,128]{1,0:T(8,128)} %bitcast.32, ...), custom_call_target="tpu_custom_call" | custom-call | flops 8153726976 | bytes 4000000 | tf_op jit(solution)/shard_map/pallas_call | solution.py:459
  69.0 1.5 %slice_bitcast_fusion = (f32[2304]{0:T(1024)}, f32[2304]{0:T(1024)}, f32[2304]{0:T(1024)}, f32[2304]{0:T(1024)}, f32[2304]{0:T(1024)}, /*index=5*/f32[2304]{0:T(1024)}, f32[2304]{0:T(1024)}, f32[2304]{0:T(1024)}) fusion(f32[8,24,128]{2,1,0:T(8,128)} %shard_map.170), kind=kLoop, calls=%fused_computation | loop fusion | bytes 147456 | tf_op jit(solution)/shard_map/reshape;squeeze | solution.py:508

commit v3 on v2

--- a/solution.py
+++ b/solution.py
@@ -20,7 +20,17 @@
 H, WD, CH = 8, 288, 256
 PIX = H * WD
 GROUPS = (1, 0, 2)
-PARTS = (((0, 1), (3, 4, 0, 1, 2), 0, 1440), ((2,), (5, 6, 7), 1440, 2304))
+ZORDER = (3, 4, 0, 1, 2, 5, 6, 7)
+PARTS = ((0, 32, 0, (768, 1536)), (32, 80, 1, (0, 768)), (80, 144, 2, (1536, 2304)))
+
+
+def pieces(lo, hi):
+    cut = []
+    for j, zz in enumerate(ZORDER):
+        first, last = max(lo, 18 * j), min(hi, 18 * j + 18)
+        if first < last:
+            cut.append((zz, first - 18 * j, last - first))
+    return cut
 
 
 def dev(z, x, y, c):
@@ -43,10 +53,10 @@
 
 
 def kernel(
-    x_hbm, p1_hbm, p2_hbm, lab, ct, w1, m1, v1, w2, m2, v2,
+    x_hbm, p1_hbm, p2_hbm, lab_hbm, ct_hbm, w1_hbm, m1_hbm, v1_hbm, w2_hbm, m2_hbm, v2_hbm,
     outs,
-    xv, p1, p2, xt, gs, c3, wsend, g0, ga_, wf, wd,
-    st, precv, tot, asend0, arecv0, asend1, arecv1, zsend, zrecv, gfin, nbuf,
+    lab, ct, w1, m1, v1, w2, m2, v2, xv, p1, p2, xt, gs, c3, wsend, g0, ga_, wf, wd,
+    st, precv, tot, asend, arecv, asum, zsend, zrecv, gfin, nbuf,
     ld, s_g0, r_g0, s_g1, r_g1, s_g2, r_g2, s_g3, r_g3, s_h, r_h,
     s_p, r_p, s_a, r_a, s_z, r_z, s_n, r_n,
 ):
@@ -64,9 +74,22 @@
     cp_p2 = pltpu.make_async_copy(p2_hbm, p2, ld.at[0])
     cp_p1 = pltpu.make_async_copy(p1_hbm, p1, ld.at[1])
     cp_x = pltpu.make_async_copy(x_hbm, xv, ld.at[2])
+    small = [
+        pltpu.make_async_copy(src, dst, ld.at[3 + i])
+        for i, (src, dst) in enumerate(
+            (
+                (w2_hbm, w2), (ct_hbm, ct), (lab_hbm, lab), (m2_hbm, m2), (v2_hbm, v2),
+                (w1_hbm, w1), (m1_hbm, m1), (v1_hbm, v1),
+            )
+        )
+    ]
+    for copy in small[:3]:
+        copy.start()
     cp_p2.start()
     cp_p1.start()
     cp_x.start()
+    for copy in small[3:]:
+        copy.start()
 
     bar = pltpu.get_barrier_semaphore()
 
@@ -81,6 +104,8 @@
     loop(1, 16, sig_zc)
     loop(1, 16, sig_xy)
 
+    for copy in small[:3]:
+        copy.wait()
     for h in (0, 1):
         wsend[h, 0:9, :] = w2[pl.ds(h, 9, stride=2), :].astype(BF)
 
@@ -234,83 +259,89 @@
             part = lax.dot_general(
                 xt[...], window, (((1,), (0,)), ((), ())), preferred_element_type=F32
             )
-            at = pl.ds(pl.multiple_of((dy * 3 + dx) * 256, 256), 256)
+            at = pl.ds((dy * 3 + dx) * 256, 256)
             st[layer, 0, at, :] = part[:, 0:128]
             st[layer, 1, at, :] = part[:, 128:256]
 
-        loop(0, 3, one)
+        for dx in range(3):
+            one(dx)
         pair_copy(layer, group).start()
 
-    def pack_refs(part):
-        return (asend0, arecv0) if part == 0 else (asend1, arecv1)
+    def spans(layer):
+        return ((0, 144),) if layer == 0 else tuple(p[:2] for p in PARTS)
 
     def a_copy(layer, part, i):
-        send, recv = pack_refs(part)
+        lo, hi = spans(layer)[part]
         k = (place + i) % 16
         return rcopy(
-            send.at[layer, k], recv.at[layer, place],
+            asend.at[layer, k, pl.ds(lo, hi - lo)], arecv.at[layer, place, pl.ds(lo, hi - lo)],
             s_a.at[layer, part, i], r_a.at[layer, part, place], dev(z, k // 4, k % 4, c),
         )
 
+    def a_sum(layer, group):
+        pair_copy(layer, group).wait_recv()
+        lo, hi = PARTS[group][3]
+        tot[lo:hi, :] = st[layer, c, lo:hi, :] + precv[layer, lo:hi, :]
+
     def a_start(layer, part):
-        for group in PARTS[part][0]:
-            pair_copy(layer, group).wait_recv()
-        _, zs, lo, hi = PARTS[part]
-        tot[lo:hi, :] = st[layer, c, lo:hi, :] + precv[layer, lo:hi, :]
-        send = pack_refs(part)[0]
-        rows = 18 * len(zs)
+        lo, hi = spans(layer)[part]
 
         def one(xx):
             base = pl.multiple_of(xx * 72, 8)
             for yy in range(NA):
                 block = jnp.concatenate(
-                    [tot[pl.ds(base + 288 * zz + 18 * yy, 18), :] for zz in zs]
-                    + [jnp.zeros((send.shape[2] - rows, 128), F32)],
+                    [
+                        tot[pl.ds(base + 288 * zz + 18 * yy + r, n), :]
+                        for zz, r, n in pieces(lo, hi)
+                    ],
                     axis=0,
                 )
-                send[layer, xx * 4 + yy] = block.astype(BF)
+                asend[layer, xx * 4 + yy, lo:hi, :] = block.astype(BF)
 
         loop(0, NA, one)
         loop(1, 16, lambda i: a_copy(layer, part, i).start())
 
-    def z_copy(layer, i):
-        k = (slot + i) % 16
+    def z_copy(layer, k):
         return rcopy(
             zsend.at[layer, k], zrecv.at[layer, slot],
-            s_z.at[layer, i], r_z.at[layer, slot], dev(k // 2, x, y, k % 2),
-        )
-
-    def a_finish(layer):
-        for part in range(2):
-            send, recv = pack_refs(part)
-
-            def wait(i, part=part, recv=recv):
-                k = (place + i) % 16
-                rcopy(
-                    recv.at[layer, k], recv.at[layer, k],
-                    s_a.at[layer, part, i], r_a.at[layer, part, k], other,
-                ).wait_recv()
-
-            loop(1, 16, wait)
-            total = lax.fori_loop(
-                1, 16,
-                lambda i, acc, recv=recv: acc + recv[layer, (place + i) % 16].astype(F32),
-                send[layer, place].astype(F32),
-            )
-            for j, zz in enumerate(PARTS[part][1]):
-                for cc in range(2):
-                    r = 18 * j + 9 * cc
-                    zsend[layer, 2 * zz + cc, 0:9, :] = total[r:r + 9]
-
-        zrecv[layer, slot] = zsend[layer, slot]
-        loop(1, 16, lambda i: z_copy(layer, i).start())
+            s_z.at[layer, k], r_z.at[layer, slot], dev(k // 2, x, y, k % 2),
+        )
+
+    def a_finish(layer, part, blocks):
+        lo, hi = spans(layer)[part]
+        rows = pl.ds(lo, hi - lo)
+
+        def wait(i):
+            k = (place + i) % 16
+            ref = arecv.at[layer, k, rows]
+            rcopy(ref, ref, s_a.at[layer, part, i], r_a.at[layer, part, k], other).wait_recv()
+
+        loop(1, 16, wait)
+        asum[rows, :] = lax.fori_loop(
+            1, 16,
+            lambda i, acc: acc + arecv[layer, (place + i) % 16, rows, :].astype(F32),
+            asend[layer, place, rows, :].astype(F32),
+        )
+        for j in blocks:
+            for cc in range(2):
+                k = 2 * ZORDER[j] + cc
+                r = 18 * j + 9 * cc
+                zsend[layer, k, 0:9, :] = asum[r:r + 9, :]
+
+                @pl.when(k == slot)
+                def _(k=k):
+                    zrecv[layer, slot] = zsend[layer, k]
+
+                @pl.when(k != slot)
+                def _(k=k):
+                    z_copy(layer, k).start()
 
     def z_finish(layer):
         def wait(i):
             k = (slot + i) % 16
             rcopy(
                 zrecv.at[layer, k], zrecv.at[layer, k],
-                s_z.at[layer, i], r_z.at[layer, k], other,
+                s_z.at[layer, k], r_z.at[layer, k], other,
             ).wait_recv()
 
         loop(1, 16, wait)
@@ -332,18 +363,20 @@
         )
         return (first_new, second_new, update)
 
-    def first_row(r):
-        total = jnp.zeros((WD, CH), F32)
+    def first_rows(r, n):
+        total = jnp.zeros((n * WD, CH), F32)
         for dy in range(3):
-            at = pl.ds(pl.multiple_of((r + 2 - dy) * WD, 32), WD)
+            at = pl.ds(pl.multiple_of((r + 2 - dy) * WD, 32), n * WD)
             for dx in range(3):
                 t = (dy * 3 + dx) * 256
                 tap = jnp.concatenate([wd[0, t:t + 256, :], wd[1, t:t + 256, :]], axis=1)
                 total = total + lax.dot_general(
                     gs[0, dx, at, :], tap, (((1,), (1,)), ((), ())), preferred_element_type=F32
                 )
-        pre = p1[pl.ds(pl.multiple_of(r * WD, 32), WD), :]
-        put_row(1, r + 1, jnp.where(pre.astype(F32) > 0, total, 0.0))
+        for j in range(n):
+            pre = p1[pl.ds(pl.multiple_of((r + j) * WD, 32), WD), :]
+            part = total[j * WD:(j + 1) * WD]
+            put_row(1, r + j + 1, jnp.where(pre.astype(F32) > 0, part, 0.0))
 
     cp_p2.wait()
     loop(0, 2, lambda i: second_row(i * (H - 1)))
@@ -361,21 +394,30 @@
     taps(0, 2)
     cp_x.wait()
     transpose_in(xv, False)
+    for copy in small[3:]:
+        copy.wait()
     g2_finish()
+    for group in range(3):
+        a_sum(0, group)
     a_start(0, 0)
-    a_start(0, 1)
     g3_copy().wait_recv()
-    loop(0, 2, lambda i: first_row(i * (H - 1)))
+    loop(0, 2, lambda i: first_rows(i * (H - 1), 1))
     halo_start(1)
-    loop(1, H - 1, first_row)
+    loop(0, 2, lambda i: first_rows(1 + 3 * i, 3))
     taps(1, 0)
     halo_finish(1)
     taps(1, 1)
+    a_sum(1, 0)
     a_start(1, 0)
     taps(1, 2)
+    a_sum(1, 1)
     a_start(1, 1)
-    a_finish(0)
-    a_finish(1)
+    a_sum(1, 2)
+    a_start(1, 2)
+    a_finish(0, 0, range(NZ))
+    a_finish(1, 0, ())
+    a_finish(1, 1, range(4))
+    a_finish(1, 2, range(4, NZ))
     m2n, v2n, u2 = moments(z_finish(0), w2[...], m2[...], v2[...])
     outs[4, 0:18, :] = m2n
     outs[5, 0:18, :] = v2n
@@ -426,9 +468,9 @@
     def done(i):
         g0_copy(i).wait_send()
         for layer in range(2):
-            for part in range(2):
+            for part in range(len(spans(layer))):
                 a_copy(layer, part, i).wait_send()
-            z_copy(layer, i).wait_send()
+            z_copy(layer, (slot + i) % 16).wait_send()
         for stage in range(2):
             n_copy(stage, i).wait_send()
 
@@ -459,9 +501,17 @@
     outs = pl.pallas_call(
         kernel,
         out_shape=jax.ShapeDtypeStruct((8, 24, 128), F32),
-        in_specs=[hb] * 3 + [vm] * 8,
+        in_specs=[hb] * 11,
         out_specs=vm,
         scratch_shapes=[
+            pltpu.VMEM((H, WD), jnp.int32),
+            pltpu.VMEM((3, CH), BF),
+            pltpu.VMEM((18, 128), F32),
+            pltpu.VMEM((18, 128), F32),
+            pltpu.VMEM((18, 128), F32),
+            pltpu.VMEM((18, 128), F32),
+            pltpu.VMEM((18, 128), F32),
+            pltpu.VMEM((18, 128), F32),
             pltpu.VMEM((PIX, CH), BF),
             pltpu.VMEM((PIX, CH), BF),
             pltpu.VMEM((PIX, CH), BF),
@@ -476,22 +526,21 @@
             pltpu.VMEM((2, 2, 2304, 128), F32),
             pltpu.VMEM((2, 2304, 128), F32),
             pltpu.VMEM((2304, 128), F32),
-            pltpu.VMEM((2, 16, 96, 128), BF),
-            pltpu.VMEM((2, 16, 96, 128), BF),
-            pltpu.VMEM((2, 16, 64, 128), BF),
-            pltpu.VMEM((2, 16, 64, 128), BF),
+            pltpu.VMEM((2, 16, 144, 128), BF),
+            pltpu.VMEM((2, 16, 144, 128), BF),
+            pltpu.VMEM((144, 128), F32),
             pltpu.VMEM((2, 16, 16, 128), F32),
             pltpu.VMEM((2, 16, 16, 128), F32),
             pltpu.VMEM((2, 18, 128), F32),
             pltpu.VMEM((2, 16, 8, 128), F32),
-            dma((3,)),
+            dma((11,)),
             dma((16,)), dma((16,)),
             dma((NA,)), dma((NA,)),
             dma((NA, NA)), dma((NA, NA)),
             dma, dma,
             dma((2, 2)), dma((2, 2)),
             dma((2, 3)), dma((2, 3)),
-            dma((2, 2, 16)), dma((2, 2, 16)),
+            dma((2, 3, 16)), dma((2, 3, 16)),
             dma((2, 16)), dma((2, 16)),
             dma((2, 16)), dma((2, 16)),
         ],

time: 70.7 us -> 66.9 us (0.946)
  Pallas kernels: 68.4 us -> 64.7 us
    pallas_call x1, Pallas kernels: 68.4 us -> 64.7 us  [body(): pl.pallas_call(kernel, out_shape=jax.ShapeDtypeStruct((8, 24, 128), F32),...]
where the time goes in v3:
time: 66.9 us; the launch traced here: 66.8 us
  Pallas kernels  64.7 us (97%)
  local copies, waits for them, and re-layouts  1.46 us (2%)
    pallas_call x1, Pallas kernels, body(): pl.pallas_call(kernel, out_shape=jax.ShapeDtypeStruct((8, 24, 128), F32),...  64.7 us
    another operation x1, local copies, waits for them, and re-layouts, body(): return tuple((outs[i, 0:18].reshape(2304) for i in range(8)))  1.46 us

profile of v3, /device:TPU:1, one launch (start us, length us, event | category | flops | bytes accessed | tf_op | source)
XLA Modules:
  0.0 66.8 jit_solution(11748219949470464362)
XLA Ops:
  0.6 64.7 %shard_map.170 = f32[8,24,128]{2,1,0:T(8,128)} custom-call(bf16[2304,256]{1,0:T(8,128)(2,1)} %bitcast.27, bf16[2304,256]{1,0:T(8,128)(2,1)} %bitcast.28, bf16[2304,256]{1,0:T(8,128)(2,1)} %bitcast.29, s32[8,288]{1,0:T(8,128)} %bitcast.30, bf16[3,256]{1,0:T(4,128)(2,1)} %bitcast.37, f32[18,128]{1,0:T(8,128)} %bitcast.31, f32[18,128]{1,0:T(8,128)} %bitcast.32, ...), custom_call_target="tpu_custom_call" | custom-call | flops 8153726976 | bytes 4000000 | tf_op jit(solution)/shard_map/pallas_call | solution.py:501
  65.3 1.5 %slice_bitcast_fusion = (f32[2304]{0:T(1024)}, f32[2304]{0:T(1024)}, f32[2304]{0:T(1024)}, f32[2304]{0:T(1024)}, f32[2304]{0:T(1024)}, /*index=5*/f32[2304]{0:T(1024)}, f32[2304]{0:T(1024)}, f32[2304]{0:T(1024)}) fusion(f32[8,24,128]{2,1,0:T(8,128)} %shard_map.170), kind=kLoop, calls=%fused_computation | loop fusion | bytes 147456 | tf_op jit(solution)/shard_map/reshape;squeeze | solution.py:557

commit v4 on v3

--- a/solution.py
+++ b/solution.py
@@ -52,10 +52,15 @@
     lax.fori_loop(lo, hi, lambda i, carry: (fn(i), carry)[1], 0)
 
 
+def each(lo, hi, fn):
+    for i in range(lo, hi):
+        fn(i)
+
+
 def kernel(
     x_hbm, p1_hbm, p2_hbm, lab_hbm, ct_hbm, w1_hbm, m1_hbm, v1_hbm, w2_hbm, m2_hbm, v2_hbm,
     outs,
-    lab, ct, w1, m1, v1, w2, m2, v2, xv, p1, p2, xt, gs, c3, wsend, g0, ga_, wf, wd,
+    lab, ct, w1, m1, v1, w2, m2, v2, xv, p1, p2, xt, gs, c3, wsend, g0, ga_, gb_, wf, wd,
     st, precv, tot, asend, arecv, asum, zsend, zrecv, gfin, nbuf,
     ld, s_g0, r_g0, s_g1, r_g1, s_g2, r_g2, s_g3, r_g3, s_h, r_h,
     s_p, r_p, s_a, r_a, s_z, r_z, s_n, r_n,
@@ -71,6 +76,19 @@
     def ab(aa, bb):
         return dev(z, (1 - c) * aa + c * bb, (1 - c) * bb + c * aa, c)
 
+    bar = pltpu.get_barrier_semaphore()
+
+    def sig_zc(i):
+        k = (z * 2 + c + i) % 16
+        pl.semaphore_signal(bar, inc=1, device_id=dev(k // 2, x, y, k % 2), device_id_type=MESH)
+
+    def sig_xy(i):
+        k = (x * 4 + y + i) % 16
+        pl.semaphore_signal(bar, inc=1, device_id=dev(z, k // 4, k % 4, c), device_id_type=MESH)
+
+    each(1, 16, sig_zc)
+    each(1, 16, sig_xy)
+
     cp_p2 = pltpu.make_async_copy(p2_hbm, p2, ld.at[0])
     cp_p1 = pltpu.make_async_copy(p1_hbm, p1, ld.at[1])
     cp_x = pltpu.make_async_copy(x_hbm, xv, ld.at[2])
@@ -91,19 +109,6 @@
     for copy in small[3:]:
         copy.start()
 
-    bar = pltpu.get_barrier_semaphore()
-
-    def sig_zc(i):
-        k = (z * 2 + c + i) % 16
-        pl.semaphore_signal(bar, inc=1, device_id=dev(k // 2, x, y, k % 2), device_id_type=MESH)
-
-    def sig_xy(i):
-        k = (x * 4 + y + i) % 16
-        pl.semaphore_signal(bar, inc=1, device_id=dev(z, k // 4, k % 4, c), device_id_type=MESH)
-
-    loop(1, 16, sig_zc)
-    loop(1, 16, sig_xy)
-
     for copy in small[:3]:
         copy.wait()
     for h in (0, 1):
@@ -123,7 +128,12 @@
 
     def g0_start():
         g0[slot] = wsend[c]
-        loop(1, 16, lambda i: g0_copy(i).start())
+        each(1, 16, lambda i: g0_copy(i).start())
+
+    other = dev(z, x, y, 1 - c)
+
+    def g3_copy(j, k):
+        return rcopy(ga_.at[j, k], gb_.at[j, k], s_g3.at[j, k], r_g3.at[j, k], other)
 
     def g1_copy(i):
         return rcopy(
@@ -140,43 +150,48 @@
             k = (slot + i) % 16
             rcopy(g0.at[k], g0.at[k], s_g0.at[i], r_g0.at[k], dev(z, x, y, c)).wait_recv()
 
-        loop(1, 16, one)
+        each(1, 16, one)
         pack = jnp.concatenate([g0[s, 0:16, :].astype(F32)[0:9] for s in range(16)], axis=0)
         ga_[a, b] = pack.astype(BF)
-        loop(1, NA, lambda i: g1_copy(i).start())
-        loop(1, NA, lambda i: g2_copy(b, i).start())
+        each(1, NA, lambda i: g1_copy(i).start())
+        each(1, NA, lambda i: g2_copy(b, i).start())
+        g3_copy(a, b).start()
 
     def g1_finish():
         for j in (1, 3, 2):
             k = (b + j) % NA
             rcopy(ga_.at[a, k], ga_.at[a, k], s_g1.at[j], r_g1.at[k], ab(a, k)).wait_recv()
-            loop(1, NA, lambda i, k=k: g2_copy(k, i).start())
-
-    other = dev(z, x, y, 1 - c)
-
-    def g3_copy():
-        return rcopy(wd.at[c], wd.at[c], s_g3, r_g3, other)
+            each(1, NA, lambda i, k=k: g2_copy(k, i).start())
+            g3_copy(a, k).start()
+
+    def unpack(pieces_of, core, half):
+        def one(xx):
+            base = pl.multiple_of(xx * 72, 8)
+            for yy in range(NA):
+                block = pieces_of[
+                    (1 - core) * xx + core * yy, (1 - core) * yy + core * xx
+                ].astype(F32)
+                for zz in range(NZ):
+                    wf[pl.ds(base + 288 * zz + 18 * yy, 18), :] = block[18 * zz:18 * zz + 18]
+
+        loop(0, NA, one)
+        wd[half] = wf[...].astype(BF)
 
     def g2_finish():
-        def wait(i):
+        for i in (1, 3, 2):
             k = (a + i) % NA
             for j in range(NA):
                 rcopy(
-                    ga_.at[k, j], ga_.at[k, j], s_g2.at[j, i], r_g2.at[k, j], ab(k, b)
+                    ga_.at[k, j], ga_.at[k, j], s_g2.at[j, i], r_g2.at[k, j], other
                 ).wait_recv()
-
-        loop(1, NA, wait)
-
-        def unpack(xx):
-            base = pl.multiple_of(xx * 72, 8)
-            for yy in range(NA):
-                block = ga_[(1 - c) * xx + c * yy, (1 - c) * yy + c * xx].astype(F32)
-                for zz in range(NZ):
-                    wf[pl.ds(base + 288 * zz + 18 * yy, 18), :] = block[18 * zz:18 * zz + 18]
-
-        loop(0, NA, unpack)
-        wd[c] = wf[...].astype(BF)
-        g3_copy().start()
+                g3_copy(k, j).start()
+        unpack(ga_, c, c)
+
+    def g3_finish():
+        for j in range(NA):
+            for k in range(NA):
+                g3_copy(j, k).wait_recv()
+        unpack(gb_, 1 - c, 1 - c)
 
     cols = lax.broadcasted_iota(jnp.int32, (WD, CH), 0)
 
@@ -299,7 +314,7 @@
                 asend[layer, xx * 4 + yy, lo:hi, :] = block.astype(BF)
 
         loop(0, NA, one)
-        loop(1, 16, lambda i: a_copy(layer, part, i).start())
+        each(1, 16, lambda i: a_copy(layer, part, i).start())
 
     def z_copy(layer, k):
         return rcopy(
@@ -316,7 +331,7 @@
             ref = arecv.at[layer, k, rows]
             rcopy(ref, ref, s_a.at[layer, part, i], r_a.at[layer, part, k], other).wait_recv()
 
-        loop(1, 16, wait)
+        each(1, 16, wait)
         asum[rows, :] = lax.fori_loop(
             1, 16,
             lambda i, acc: acc + arecv[layer, (place + i) % 16, rows, :].astype(F32),
@@ -344,7 +359,7 @@
                 s_z.at[layer, k], r_z.at[layer, k], other,
             ).wait_recv()
 
-        loop(1, 16, wait)
+        each(1, 16, wait)
         for cc in range(2):
             total = zrecv[layer, cc, 0:9, :]
             for zz in range(1, NZ):
@@ -400,7 +415,7 @@
     for group in range(3):
         a_sum(0, group)
     a_start(0, 0)
-    g3_copy().wait_recv()
+    g3_finish()
     loop(0, 2, lambda i: first_rows(i * (H - 1), 1))
     halo_start(1)
     loop(0, 2, lambda i: first_rows(1 + 3 * i, 3))
@@ -452,11 +467,11 @@
         ref = nbuf.at[stage, k]
         rcopy(ref, ref, s_n.at[stage, i], r_n.at[stage, k], other).wait_recv()
 
-    loop(1, 16, lambda i: n_copy(0, i).start())
-    loop(1, 16, lambda i: n_wait(0, i))
+    each(1, 16, lambda i: n_copy(0, i).start())
+    each(1, 16, lambda i: n_wait(0, i))
     nbuf[1, place] = jnp.sum(nbuf[0], axis=0)
-    loop(1, 16, lambda i: n_copy(1, i).start())
-    loop(1, 16, lambda i: n_wait(1, i))
+    each(1, 16, lambda i: n_copy(1, i).start())
+    each(1, 16, lambda i: n_wait(1, i))
     sums = jnp.sqrt(jnp.sum(jnp.sum(nbuf[1], axis=0), axis=1, keepdims=True))
     step1 = sums[0:1] / sums[1:2] * u1
     step2 = sums[2:3] / sums[3:4] * u2
@@ -474,15 +489,17 @@
         for stage in range(2):
             n_copy(stage, i).wait_send()
 
-    loop(1, 16, done)
+    each(1, 16, done)
 
     def done_gather(i):
         g1_copy(i).wait_send()
         for k in range(NA):
             g2_copy(k, i).wait_send()
 
-    loop(1, NA, done_gather)
-    g3_copy().wait_send()
+    each(1, NA, done_gather)
+    for j in range(NA):
+        for k in range(NA):
+            g3_copy(j, k).wait_send()
     for layer in range(2):
         halo_copy(layer, True).wait_send()
         halo_copy(layer, False).wait_send()
@@ -521,6 +538,7 @@
             pltpu.VMEM((2, 16, 128), BF),
             pltpu.VMEM((16, 16, 128), BF),
             pltpu.VMEM((NA, NA, 144, 128), BF),
+            pltpu.VMEM((NA, NA, 144, 128), BF),
             pltpu.VMEM((2304, 128), F32),
             pltpu.VMEM((2, 2304, 128), BF),
             pltpu.VMEM((2, 2, 2304, 128), F32),
@@ -537,7 +555,7 @@
             dma((16,)), dma((16,)),
             dma((NA,)), dma((NA,)),
             dma((NA, NA)), dma((NA, NA)),
-            dma, dma,
+            dma((NA, NA)), dma((NA, NA)),
             dma((2, 2)), dma((2, 2)),
             dma((2, 3)), dma((2, 3)),
             dma((2, 3, 16)), dma((2, 3, 16)),

time: 66.9 us -> 66.2 us (0.990)
  Pallas kernels: 64.7 us -> 63.9 us
    pallas_call x1, Pallas kernels: 64.7 us -> 63.9 us  [body(): pl.pallas_call(kernel, out_shape=jax.ShapeDtypeStruct((8, 24, 128), F32),...]
where the time goes in v4:
time: 66.2 us; the launch traced here: 66 us
  Pallas kernels  63.9 us (97%)
  local copies, waits for them, and re-layouts  1.46 us (2%)
    pallas_call x1, Pallas kernels, body(): pl.pallas_call(kernel, out_shape=jax.ShapeDtypeStruct((8, 24, 128), F32),...  63.9 us
    another operation x1, local copies, waits for them, and re-layouts, body(): return tuple((outs[i, 0:18].reshape(2304) for i in range(8)))  1.46 us

profile of v4, /device:TPU:1, one launch (start us, length us, event | category | flops | bytes accessed | tf_op | source)
XLA Modules:
  0.0 66.0 jit_solution(14097726342242373293)
XLA Ops:
  0.6 63.9 %shard_map.170 = f32[8,24,128]{2,1,0:T(8,128)} custom-call(bf16[2304,256]{1,0:T(8,128)(2,1)} %bitcast.27, bf16[2304,256]{1,0:T(8,128)(2,1)} %bitcast.28, bf16[2304,256]{1,0:T(8,128)(2,1)} %bitcast.29, s32[8,288]{1,0:T(8,128)} %bitcast.30, bf16[3,256]{1,0:T(4,128)(2,1)} %bitcast.37, f32[18,128]{1,0:T(8,128)} %bitcast.31, f32[18,128]{1,0:T(8,128)} %bitcast.32, ...), custom_call_target="tpu_custom_call" | custom-call | flops 8153726976 | bytes 4000000 | tf_op jit(solution)/shard_map/pallas_call | solution.py:518
  64.5 1.5 %slice_bitcast_fusion = (f32[2304]{0:T(1024)}, f32[2304]{0:T(1024)}, f32[2304]{0:T(1024)}, f32[2304]{0:T(1024)}, f32[2304]{0:T(1024)}, /*index=5*/f32[2304]{0:T(1024)}, f32[2304]{0:T(1024)}, f32[2304]{0:T(1024)}) fusion(f32[8,24,128]{2,1,0:T(8,128)} %shard_map.170), kind=kLoop, calls=%fused_computation | loop fusion | bytes 147456 | tf_op jit(solution)/shard_map/reshape;squeeze | solution.py:575

commit v5 on v4

--- a/solution.py
+++ b/solution.py
@@ -50,6 +50,10 @@
 
 def loop(lo, hi, fn):
     lax.fori_loop(lo, hi, lambda i, carry: (fn(i), carry)[1], 0)
+
+
+def aligned(at, step):
+    return at if isinstance(at, int) else pl.multiple_of(at, step)
 
 
 def each(lo, hi, fn):
@@ -274,12 +278,14 @@
             part = lax.dot_general(
                 xt[...], window, (((1,), (0,)), ((), ())), preferred_element_type=F32
             )
-            at = pl.ds((dy * 3 + dx) * 256, 256)
+            at = pl.ds(aligned((dy * 3 + dx) * 256, 256), 256)
             st[layer, 0, at, :] = part[:, 0:128]
             st[layer, 1, at, :] = part[:, 128:256]
 
-        for dx in range(3):
-            one(dx)
+        if layer == 0:
+            loop(0, 3, one)
+        else:
+            each(0, 3, one)
         pair_copy(layer, group).start()
 
     def spans(layer):
@@ -411,10 +417,10 @@
     transpose_in(xv, False)
     for copy in small[3:]:
         copy.wait()
-    g2_finish()
     for group in range(3):
         a_sum(0, group)
     a_start(0, 0)
+    g2_finish()
     g3_finish()
     loop(0, 2, lambda i: first_rows(i * (H - 1), 1))
     halo_start(1)

time: 66.2 us -> 66.3 us (level)
  no operation moved by 1% of the time
where the time goes in v5:
time: 66.3 us; the launch traced here: 66.1 us
  Pallas kernels  64 us (97%)
  local copies, waits for them, and re-layouts  1.46 us (2%)
    pallas_call x1, Pallas kernels, body(): pl.pallas_call(kernel, out_shape=jax.ShapeDtypeStruct((8, 24, 128), F32),...  64 us
    another operation x1, local copies, waits for them, and re-layouts, body(): return tuple((outs[i, 0:18].reshape(2304) for i in range(8)))  1.46 us

profile of v5, /device:TPU:1, one launch (start us, length us, event | category | flops | bytes accessed | tf_op | source)
XLA Modules:
  0.0 66.1 jit_solution(10547830389156046040)
XLA Ops:
  0.6 64.0 %shard_map.170 = f32[8,24,128]{2,1,0:T(8,128)} custom-call(bf16[2304,256]{1,0:T(8,128)(2,1)} %bitcast.27, bf16[2304,256]{1,0:T(8,128)(2,1)} %bitcast.28, bf16[2304,256]{1,0:T(8,128)(2,1)} %bitcast.29, s32[8,288]{1,0:T(8,128)} %bitcast.30, bf16[3,256]{1,0:T(4,128)(2,1)} %bitcast.37, f32[18,128]{1,0:T(8,128)} %bitcast.31, f32[18,128]{1,0:T(8,128)} %bitcast.32, ...), custom_call_target="tpu_custom_call" | custom-call | flops 8153726976 | bytes 4000000 | tf_op jit(solution)/shard_map/pallas_call | solution.py:524
  64.6 1.5 %slice_bitcast_fusion = (f32[2304]{0:T(1024)}, f32[2304]{0:T(1024)}, f32[2304]{0:T(1024)}, f32[2304]{0:T(1024)}, f32[2304]{0:T(1024)}, /*index=5*/f32[2304]{0:T(1024)}, f32[2304]{0:T(1024)}, f32[2304]{0:T(1024)}) fusion(f32[8,24,128]{2,1,0:T(8,128)} %shard_map.170), kind=kLoop, calls=%fused_computation | loop fusion | bytes 147456 | tf_op jit(solution)/shard_map/reshape;squeeze | solution.py:581
